TPU v7x, 32 devices: a whole 2x2x4 slice. The times are simulated.
32 devices in a mesh: replica: 2 (over x), node: 8 (over z, y), local: 2 (over core).
Axes of the slice: x: 2, y: 2, z: 4, core: 2. Of those that a mesh axis runs over, the one named last changes fastest.
Arguments:
- gate_pre: bfloat16 [2048, 14336], P(('replica', 'node'), 'local'), may hold values from -6 to 6
- up_pre: bfloat16 [2048, 14336], P(('replica', 'node'), 'local'), may hold values from -6 to 6
- upstream: bfloat16 [2048, 4096], P(('replica', 'node')), may hold values from -6 to 6
- weight_codes: bfloat16 [4096, 14336], P('node', 'local'), may hold values from -0.046875 to 0.046875
- scales: bfloat16 [4096, 112], P('node', 'local'), may hold values from 0.5 to 4
Outputs:
- layer_out: bfloat16 [2048, 4096], P(('replica', 'node', 'local'))
- gate_grad: bfloat16 [2048, 14336], P(('replica', 'node'), 'local')
- up_grad: bfloat16 [2048, 14336], P(('replica', 'node'), 'local')
- weight_grad: bfloat16 [4096, 14336], P(('replica', 'node'), 'local')
All inputs are finite; a program needn't handle non-finite values.
Results may differ from a plain program's by a relative error of at most 0.013.
Values may be sent and summed in bfloat16 or wider, within the bound.
No kernel may reach another device: no remote copies, remote signals or barrier semaphores. Data moves between devices by JAX's collectives and lax.ppermute only.
A program may use at most 384 MiB of HBM per device.

v0:
```python
import functools

import jax
import jax.numpy as jnp
from jax import lax
from jax.experimental import pallas as pl
from jax.experimental.pallas import tpu as pltpu
from jax.sharding import Mesh, PartitionSpec as P

LINK = jnp.bfloat16


def contract(left, right, left_dim, right_dim):
    return lax.dot_general(
        left, right, (((left_dim,), (right_dim,)), ((), ())), preferred_element_type=jnp.float32
    )


def project_body(steps, left_ref, *refs):
    *right_refs, out_ref, total_ref = refs
    step = pl.program_id(1)

    @pl.when(step == 0)
    def _():
        total_ref[...] = jnp.zeros_like(total_ref)

    for h, right_ref in enumerate(right_refs):

        @pl.when(lax.div(step, steps) == h)
        def _(right_ref=right_ref):
            total_ref[...] += contract(left_ref[...], right_ref[...], 1, 1)

    @pl.when(step == pl.num_programs(1) - 1)
    def _():
        out_ref[...] = total_ref[...].astype(out_ref.dtype)


def project(left, rights):
    rows = left.shape[0]
    columns, width = rights[0].shape
    row_tile, tile = 512, width // 2
    if tile % 128 or rows % row_tile or columns % 128:
        return contract(left, jnp.concatenate(rights, axis=1), 1, 1).astype(LINK)
    steps = width // tile
    flops = 2 * rows * columns * width * len(rights)
    return pl.pallas_call(
        functools.partial(project_body, steps),
        out_shape=jax.ShapeDtypeStruct((rows, columns), LINK),
        grid=(rows // row_tile, steps * len(rights)),
        in_specs=[pl.BlockSpec((row_tile, tile), lambda i, k: (i, k))]
        + [
            pl.BlockSpec((columns, tile), lambda i, k, h=h: (0, jnp.clip(k - h * steps, 0, steps - 1)))
            for h in range(len(rights))
        ],
        out_specs=pl.BlockSpec((row_tile, columns), lambda i, k: (i, 0)),
        scratch_shapes=[pltpu.VMEM((row_tile, columns), jnp.float32)],
        cost_estimate=pl.CostEstimate(flops=flops, bytes_accessed=flops // 256, transcendentals=0),
        compiler_params=pltpu.CompilerParams(vmem_limit_bytes=24 * 1024 * 1024),
    )(left, *rights)


def after(value, *others):
    return lax.optimization_barrier((value, *others))[0]


def scale_body(block, index_ref, codes_ref, scales_ref, out_ref):
    shape = (scales_ref.shape[1], codes_ref.shape[1])
    unit = lax.broadcasted_iota(jnp.int32, shape, 1) + index_ref[pl.program_id(0)] * shape[1]
    first = lax.broadcasted_iota(jnp.int32, shape, 0) * block
    owned = jnp.where((unit >= first) & (unit < first + block), 1.0, 0.0).astype(jnp.bfloat16)
    spread = jnp.dot(scales_ref[...], owned, preferred_element_type=jnp.float32)
    out_ref[...] = (codes_ref[...].astype(jnp.float32) * spread).astype(jnp.bfloat16)


def dequantize_pieces(codes, scales, indices, piece, slots=1, slot=0):
    rows = codes.shape[0]
    block = codes.shape[1] // scales.shape[1]
    if piece % 128 or rows % 256:
        whole = codes.astype(jnp.float32) * jnp.repeat(scales.astype(jnp.float32), block, axis=1)
        parts = [lax.dynamic_slice_in_dim(whole, i * piece, piece, 1) for i in indices]
        parts = jnp.concatenate(parts, axis=1).astype(jnp.bfloat16)
        return lax.dynamic_update_slice_in_dim(
            jnp.zeros((slots * rows, parts.shape[1]), jnp.bfloat16), parts, slot * rows, 0
        )
    count, tile = len(indices), 256
    return pl.pallas_call(
        functools.partial(scale_body, block),
        out_shape=jax.ShapeDtypeStruct((slots * rows, count * piece), jnp.bfloat16),
        grid_spec=pltpu.PrefetchScalarGridSpec(
            num_scalar_prefetch=1,
            grid=(count, rows // tile),
            in_specs=[
                pl.BlockSpec((tile, piece), lambda i, r, index: (r, index[i])),
                pl.BlockSpec((tile, scales.shape[1]), lambda i, r, index: (r, 0)),
            ],
            out_specs=pl.BlockSpec(
                (tile, piece), lambda i, r, index: (index[count] * (rows // tile) + r, i)
            ),
        ),
        cost_estimate=pl.CostEstimate(
            flops=rows * count * piece, bytes_accessed=4 * rows * count * piece, transcendentals=0
        ),
    )(jnp.stack([*indices, jnp.asarray(slot)]).astype(jnp.int32), codes, scales)


def per_device(gate_pre, up_pre, upstream, weight_codes, scales):
    copies, depth, pairs, cores = (lax.axis_size(name) for name in ("replica", "z", "y", "local"))
    x, z, y, core = (lax.axis_index(name) for name in ("replica", "z", "y", "local"))
    above = depth - 1 - z
    tok_rows, feature_count = upstream.shape
    node_rows, unit_count = weight_codes.shape
    halves = 2
    piece = unit_count // (copies * pairs * halves)
    part_units = piece * halves
    chain_units = piece * copies
    plane_rows = node_rows * pairs
    owned_rows = feature_count // (copies * depth * pairs)
    core_rows = tok_rows // cores
    block = unit_count // scales.shape[1]
    group_rows = pairs * tok_rows

    def send_ring(value, axis, size, shift):
        if shift % size == 0:
            return value
        return lax.ppermute(value, axis, [(i, (i + shift) % size) for i in range(size)])

    def send_plane(value, dx, dy):
        moves = [
            (a * pairs + b, ((a + dx) % copies) * pairs + (b + dy) % pairs)
            for a in range(copies)
            for b in range(pairs)
        ]
        return lax.ppermute(value, ("replica", "y"), moves) if (dx, dy) != (0, 0) else value

    def send_lines(up_value, down_value, sources):
        last = depth - 1
        ups = [(i, i + 1) for i in sources]
        downs = [(last - i, last - i - 1) for i in sources]
        ends = {j for _, j in ups}
        apart = not ({i for i, _ in ups} & {i for i, _ in downs}) and not (ends & {j for _, j in downs})
        if not apart:
            return lax.ppermute(up_value, "z", ups), lax.ppermute(down_value, "z", downs)
        first = min(ends)
        if first < depth - first - 1:
            is_up, to_up = z <= max(i for i, _ in ups), z <= max(ends)
        else:
            is_up, to_up = z >= min(i for i, _ in ups), z >= first
        moved = lax.ppermute(jnp.where(is_up, up_value, down_value), "z", ups + downs)
        none = jnp.zeros_like(moved)
        return jnp.where(to_up, moved, none), jnp.where(to_up, none, moved)

    def quarter(dx, dy):
        return lax.rem(y + dy + pairs, pairs) * copies + lax.rem(x + dx + copies, copies)

    def columns(value, index, width):
        return lax.dynamic_slice_in_dim(value, index * width, width, 1)

    def of_quarter(value, dx):
        return jnp.concatenate(
            [value[:, (h * copies + dx) * piece : (h * copies + dx + 1) * piece] for h in range(halves)], axis=1
        )

    near = jnp.minimum(z, above)

    def arrival(j):
        both = j <= 2 * near
        distance = jnp.where(both, (j + 1) // 2, j - near)
        below = jnp.where(both, j % 2 == 1, z > above)
        return distance, below

    def arrival_plane(j):
        distance, below = arrival(j)
        return jnp.where(below, z - distance, z + distance)

    def arrival_index(plane):
        distance = jnp.abs(plane - z)
        return jnp.where(
            distance <= near, 2 * distance - (plane < z).astype(jnp.int32), near + distance
        )

    def hidden_part(dy):
        parts = []
        for h in range(halves):
            for dx in range(copies):
                index = quarter(dx, dy) * halves + h
                gate_value = columns(gate_pre, index, piece).astype(jnp.float32)
                up_value = columns(up_pre, index, piece).astype(jnp.float32)
                parts.append((gate_value * jax.nn.sigmoid(gate_value) * up_value).astype(jnp.bfloat16))
        return jnp.concatenate(parts, axis=1)

    hidden_parts = [hidden_part(dy) for dy in range(pairs)]
    groups = [send_ring(part, "y", pairs, dy) for dy, part in enumerate(hidden_parts)]

    core_up = lax.dynamic_slice_in_dim(after(upstream, *hidden_parts[1:]), core * core_rows, core_rows, 0)

    def plane_features(plane):
        per_copy = pairs * owned_rows
        return jnp.concatenate(
            [lax.dynamic_slice_in_dim(core_up, plane * plane_rows, plane_rows, 1)]
            + [
                lax.dynamic_slice_in_dim(core_up, (copy * depth + plane) * per_copy, per_copy, 1)
                for copy in range(copies)
            ],
            axis=1,
        )

    along = [plane_features(z)]
    for shift in range(1, depth):
        along.append(send_ring(plane_features(lax.rem(z + shift, depth)), "z", depth, shift))
    along = jnp.stack(along)

    def weight_parts(places, h, codes, *slots):
        indices = [quarter(dx, dy) * halves + h for dx, dy in places]
        return dequantize_pieces(codes, scales, indices, piece, *slots)

    given = [[weight_parts([(0, dy)], h, weight_codes) for dy in range(1, pairs)] for h in range(halves)]
    own = [weight_parts([(dx, 0) for dx in range(copies)], h, after(weight_codes, given[0][0]), pairs, y) for h in range(halves)]
    early = send_lines(*(after(groups[0], along),) * 2, range(depth - 1))
    groups = [groups[0]] + after(groups[1:], *own, *given[1])
    steps = [(jnp.concatenate(groups, axis=0),) * 2]

    up_own = along[:, :, :plane_rows]
    rows = []
    for h in range(halves):
        rows_h = [own[h]]
        for dy in range(1, pairs):
            ready = after(given[h][dy - 1], *([around[1]] if h else []))
            ready = send_ring(ready, "y", pairs, dy)
            if h == 0:
                ready = after(ready, steps[0][0])
                up_own = after(up_own, ready)
                around = [send_ring(up_own, "y", pairs, shift) for shift in range(pairs)]
            passed = [ready] + [send_ring(ready, "replica", copies, -dx) for dx in range(1, copies)]
            rows_h.append(passed)
        rows.append(rows_h)

    late = [send_lines(group, group, range(depth - 1)) for group in after(groups[1:], *early)]
    steps.append(tuple(jnp.concatenate([early[side]] + [v[side] for v in late], axis=0) for side in range(2)))
    for step in range(2, depth):
        steps.append(send_lines(*steps[-1], range(step - 1, depth - 1)))

    around = jnp.stack(around, axis=1)
    whole = jnp.zeros((depth, pairs, cores, core_rows, plane_rows), jnp.bfloat16)
    for shift in range(cores):
        whole = lax.dynamic_update_slice_in_dim(
            whole,
            send_ring(around, "local", cores, shift)[:, :, None],
            lax.rem(core - shift + cores, cores),
            2,
        )
    up_weight = whole.reshape(depth * group_rows, plane_rows)

    weight, partial = [], []
    for h in range(halves):
        half = rows[h][0]
        for dy in range(1, pairs):
            row = lax.rem(y - dy + pairs, pairs) * node_rows
            for dx, part in enumerate(rows[h][dy]):
                half = lax.dynamic_update_slice(half, part, (row, dx * piece))
        weight.append(half)
        product = contract(up_weight if h else after(up_weight, *steps[1]), weight[h], 1, 0).astype(LINK)
        partial.append(product.reshape(depth, group_rows, chain_units))

    up_sums = after(along[:, :, plane_rows:], *rows[0][1])
    up_sums = jnp.stack([send_ring(up_sums, "replica", copies, dx) for dx in range(copies)], axis=1)
    up_sums = jnp.stack([send_ring(up_sums, "y", pairs, dy) for dy in range(pairs)], axis=2)


    arrived = [steps[0][0]]
    for j in range(1, depth):
        distance, below = arrival(j)
        value = None
        for d in range((j + 1) // 2, j + 1):
            came = after(steps[d], arrived[j - 1])
            pick = jnp.where(below, came[0], came[1])
            value = pick if value is None else jnp.where(distance == d, pick, value)
        arrived.append(value)

    crossed = []
    for j in range(depth):
        ready = after(arrived[j], *(crossed[-1] if j else rows[1][1]), partial[0])
        ready = [of_quarter(ready, dx) for dx in range(copies)]
        crossed.append([send_ring(part, "replica", copies, dx) for dx, part in enumerate(ready)])
    hidden_quarter = jnp.concatenate([part for parts in crossed for part in parts], axis=0)

    up_sums = after(up_sums, *steps[depth - 1])
    whole = jnp.zeros((depth, copies, pairs, cores, core_rows, plane_rows), jnp.bfloat16)
    for shift in range(cores):
        whole = lax.dynamic_update_slice_in_dim(
            whole,
            send_ring(up_sums, "local", cores, shift)[:, :, :, None],
            lax.rem(core - shift + cores, cores),
            3,
        )
    up_sums = jnp.concatenate(
        [
            lax.dynamic_index_in_dim(whole, lax.rem(z - arrival_plane(j) + depth, depth), 0, keepdims=False)
            for j in range(depth)
        ]
    ).reshape(-1, plane_rows)

    def own_partial(goal):
        index = lax.rem(z - goal + depth, depth)
        return [lax.dynamic_index_in_dim(part, index, 0, keepdims=False) for part in partial]

    goals = [(jnp.clip(depth - step + z, 0, depth - 1), jnp.clip(step + z - depth, 0, depth - 1)) for step in range(depth)]
    first = own_partial(jnp.where(2 * z < depth, *goals[1]))
    first = [send_lines(value, value, range(1)) for value in first]
    sums = [jnp.concatenate([v[side] for v in first], axis=1) for side in range(2)]
    for step in range(2, depth):
        if step == depth - 2:
            sums = after(sums, *steps[depth - 2])
        going = [jnp.concatenate(own_partial(goals[step][side]), axis=1) + sums[side] for side in range(2)]
        if step < depth - 1:
            sums = send_lines(*going, range(step))

    out = project(after(jnp.concatenate(arrived, axis=0), *crossed[1], *crossed[2], *ready), weight)
    out = out.reshape(depth, pairs, cores, core_rows, plane_rows)
    total = lax.dynamic_index_in_dim(out, core, 2, keepdims=False).astype(jnp.float32)
    for shift in range(1, cores):
        target = lax.rem(core + shift, cores)
        total += send_ring(
            lax.dynamic_index_in_dim(out, target, 2, keepdims=False), "local", cores, shift
        ).astype(jnp.float32)
    total = total.astype(LINK)
    mine = sum(send_ring(total[:, g], "y", pairs, -g).astype(jnp.float32) for g in range(pairs)).astype(LINK)

    grads = (contract(up_sums, after(hidden_quarter), 0, 0) / float(copies)).astype(jnp.bfloat16)

    sums = []
    for h in range(halves):
        part = [value[:, h * chain_units : (h + 1) * chain_units] for value in going]
        sums.append(send_lines(*after(part, *(sums[0] if h else (out, grads))), range(depth - 1)))

    grads = grads.reshape(copies * pairs, owned_rows, part_units)
    weight_grad = jnp.zeros((owned_rows, unit_count), jnp.bfloat16)
    owned = []
    for dx in range(copies):
        for dy in range(pairs):
            chip = lax.rem(x + dx, copies) * pairs + lax.rem(y + dy, pairs)
            part = send_plane(lax.dynamic_index_in_dim(grads, chip, 0, keepdims=False), dx, dy)
            owned.append(part)
            weight_grad = lax.dynamic_update_slice_in_dim(
                weight_grad, part, quarter(-dx, -dy) * part_units, 1
            )

    own_sums = own_partial(z)
    returned = []
    for h in range(halves):
        total = sum(v.astype(jnp.float32) for v in (*after(sums[h], *owned[1 + 2 * h : 3 + h]), own_sums[h]))
        back = total.astype(LINK).reshape(pairs, tok_rows, chain_units)
        returned.append([send_ring(back[g], "y", pairs, -g) for g in range(pairs)])

    mine = after(mine, *sums[1])
    layer_out = jnp.zeros((core_rows, feature_count), jnp.bfloat16)
    for k in range(depth):
        plane = lax.rem(z - k + depth, depth)
        part = lax.dynamic_index_in_dim(mine, arrival_index(plane), 0, keepdims=False)
        part = send_ring(part, "z", depth, -k)
        layer_out = lax.dynamic_update_slice_in_dim(
            layer_out, part, lax.rem(z + k, depth) * plane_rows, 1
        )

    gate_grad = jnp.zeros((tok_rows, unit_count), jnp.bfloat16)
    up_grad = jnp.zeros((tok_rows, unit_count), jnp.bfloat16)
    for g in range(pairs):
        for h in range(halves):
            whole_part = returned[h][g]
            for dx in range(copies):
                index = quarter(dx, g) * halves + h
                part = whole_part[:, dx * piece : (dx + 1) * piece].astype(jnp.float32)
                gate_value = columns(gate_pre, index, piece).astype(jnp.float32)
                up_value = columns(up_pre, index, piece).astype(jnp.float32)
                gate_sig = jax.nn.sigmoid(gate_value)
                gate_part = part * up_value * gate_sig * (1.0 + gate_value * (1.0 - gate_sig))
                up_part = part * gate_value * gate_sig
                start = index * piece
                gate_grad = lax.dynamic_update_slice_in_dim(gate_grad, gate_part.astype(jnp.bfloat16), start, 1)
                up_grad = lax.dynamic_update_slice_in_dim(up_grad, up_part.astype(jnp.bfloat16), start, 1)
    return (layer_out, gate_grad, up_grad, weight_grad)


def solution(mesh):
    copies, nodes, cores = (mesh.shape[name] for name in ("replica", "node", "local"))
    pairs = 2
    inner = Mesh(
        mesh.devices.reshape(copies, nodes // pairs, pairs, cores), ("replica", "z", "y", "local")
    )
    tokens = ("replica", "z", "y")
    in_specs = (
        P(tokens, "local"),
        P(tokens, "local"),
        P(tokens, None),
        P(("z", "y"), "local"),
        P(("z", "y"), "local"),
    )
    out_specs = (
        P(("replica", "z", "y", "local"), None),
        P(tokens, "local"),
        P(tokens, "local"),
        P(tokens, "local"),
    )
    return jax.shard_map(
        per_device, mesh=inner, in_specs=in_specs, out_specs=out_specs, check_vma=False
    )
```

profile of v0, /device:TPU:0, one launch (start us, length us, event | category | flops | bytes accessed | tf_op | source)
XLA Modules:
  0.0 286.1 jit_solution(5971782287821418183)
XLA Ops:
  0.7 3.3 %fusion.6 = (bf16[128,896]{1,0:T(8,128)(2,1)S(1)}, bf16[128,896]{1,0:T(8,128)(2,1)S(1)}, bf16[128,896]{1,0:T(8,128)(2,1)S(1)}, bf16[128,896]{1,0:T(8,128)(2,1)S(...) fusion(bf16[128,7168]{1,0:T(8,128)(2,1)} %param.6, ...), kind=kLoop, calls=%fused_computation.118 | loop fusion | flops 7340032 | bytes 5505056 | tf_op jit(solution)/shard_map/convert_element_type | solution.py:188
  5.0 3.0 %collective-permute-start = (bf16[128,3584]{1,0:T(8,128)(2,1)}, bf16[128,3584]{1,0:T(8,128)(2,1)S(1)}, u32[]{:S(2)}, u32[]{:S(2)}) collective-permute-start(bf16[128,3584]{1,0:T(8,128)(2,1)} %pad_maximum_fusion.8), channel_id=1, source_target_pairs={{0,2},{2,0},{1,3},{3,1},{4,6},{6,4},{5,7},{7,5},{8,10},{10,8},{9,1... | collective-permute-start | bytes 2752520 | tf_op jit(solution)/shard_map/ppermute | solution.py:125
  9.3 3.7 %collective-permute-start.3 = (bf16[64,2048]{1,0:T(8,128)(2,1)S(1)}, bf16[64,2048]{1,0:T(8,128)(2,1)}, u32[]{:S(2)}, u32[]{:S(2)}) collective-permute-start(bf16[64,2048]{1,0:T(8,128)(2,1)S(1)} %pad_maximum_fusion.20), channel_id=1, source_target_pairs={{0,12},{4,0},{8,4},{12,8},{1,13},{5,1},{9,5},{13,9},{2,14},{6,2},{... | collective-permute-start | bytes 786440 | tf_op jit(solution)/shard_map/ppermute | solution.py:125
  17.0 3.1 %shard_map.84 = bf16[512,896]{1,0:T(8,128)(2,1)} custom-call(s32[2]{0:T(128)} %pad_add_fusion.1.index_ref, bf16[512,7168]{1,0:T(8,128)(2,1)} %codes_ref.5, bf16[512,56]{1,0:T(8,128)(2,1)} %copy.14.scales_ref), custom_call_target="tpu_custom_call" | custom-call | flops 458752 | bytes 1835008 | tf_op jit(solution)/shard_map/pallas_call | solution.py:86
  23.8 3.0 %shard_map.87 = bf16[512,896]{1,0:T(8,128)(2,1)} custom-call(s32[2]{0:T(128)} %pad_add_fusion.index_ref, bf16[512,7168]{1,0:T(8,128)(2,1)} %codes_ref.5, bf16[512,56]{1,0:T(8,128)(2,1)} %copy.14.scales_ref), custom_call_target="tpu_custom_call" | custom-call | flops 458752 | bytes 1835008 | tf_op jit(solution)/shard_map/pallas_call | solution.py:86
  26.9 4.8 %shard_map.85 = bf16[1024,1792]{1,0:T(8,128)(2,1)} custom-call(s32[3]{0:T(128)} %add_add_fusion.index_ref, bf16[512,7168]{1,0:T(8,128)(2,1)} %codes_ref.5, bf16[512,56]{1,0:T(8,128)(2,1)} %copy.14.scales_ref), custom_call_target="tpu_custom_call" | custom-call | flops 917504 | bytes 3670016 | tf_op jit(solution)/shard_map/pallas_call | solution.py:86
  31.7 5.0 %shard_map.86 = bf16[1024,1792]{1,0:T(8,128)(2,1)} custom-call(s32[3]{0:T(128)} %add_add_fusion.1.index_ref, bf16[512,7168]{1,0:T(8,128)(2,1)} %codes_ref.5, bf16[512,56]{1,0:T(8,128)(2,1)} %copy.14.scales_ref), custom_call_target="tpu_custom_call" | custom-call | flops 917504 | bytes 3670016 | tf_op jit(solution)/shard_map/pallas_call | solution.py:86
  38.1 4.4 %collective-permute-start.4 = (bf16[128,3584]{1,0:T(8,128)(2,1)S(1)}, bf16[128,3584]{1,0:T(8,128)(2,1)S(1)}, u32[]{:S(2)}, u32[]{:S(2)}) collective-permute-start(bf16[128,3584]{1,0:T(8,128)(2,1)S(1)} %copy-done.20), channel_id=1, source_target_pairs={{0,4},{4,8},{8,12},{1,5},{5,9},{9,13},{2,6},{6,10},{10,14},{3,7},{... | collective-permute-start | bytes 2752520 | tf_op jit(solution)/shard_map/ppermute | solution.py:142
  44.1 4.1 %collective-permute-done.11 = bf16[512,896]{1,0:T(8,128)(2,1)S(1)} collective-permute-done((bf16[512,896]{1,0:T(8,128)(2,1)}, bf16[512,896]{1,0:T(8,128)(2,1)S(1)}, u32[]{:S(2)}, u32[]{:S(2)}) %collective-permute-start.11) | collective-permute-done | bytes 917536 | tf_op jit(solution)/shard_map/ppermute | solution.py:125
  48.2 1.7 collective-permute-start.16
  52.6 8.4 %collective-permute-done.4 = bf16[128,3584]{1,0:T(8,128)(2,1)S(1)} collective-permute-done((bf16[128,3584]{1,0:T(8,128)(2,1)S(1)}, bf16[128,3584]{1,0:T(8,128)(2,1)S(1)}, u32[]{:S(2)}, u32[]{:S(2)}) %collective-permute-start.4) | collective-permute-done | bytes 917536 | tf_op jit(solution)/shard_map/ppermute | solution.py:142
  61.0 4.2 %collective-permute-done.5 = bf16[128,3584]{1,0:T(8,128)(2,1)S(1)} collective-permute-done((bf16[128,3584]{1,0:T(8,128)(2,1)S(1)}, bf16[128,3584]{1,0:T(8,128)(2,1)S(1)}, u32[]{:S(2)}, u32[]{:S(2)}) %collective-permute-start.5) | collective-permute-done | bytes 917536 | tf_op jit(solution)/shard_map/ppermute | solution.py:142
  65.2 2.2 collective-permute-start.6
  72.4 12.5 %collective-permute-done.6 = bf16[128,3584]{1,0:T(8,128)(2,1)S(1)} collective-permute-done((bf16[128,3584]{1,0:T(8,128)(2,1)S(1)}, bf16[128,3584]{1,0:T(8,128)(2,1)S(1)}, u32[]{:S(2)}, u32[]{:S(2)}) %collective-permute-start.6) | collective-permute-done | bytes 917536 | tf_op jit(solution)/shard_map/ppermute | solution.py:142
  85.7 3.3 %collective-permute-done.7 = bf16[128,3584]{1,0:T(8,128)(2,1)S(1)} collective-permute-done((bf16[128,3584]{1,0:T(8,128)(2,1)S(1)}, bf16[128,3584]{1,0:T(8,128)(2,1)S(1)}, u32[]{:S(2)}, u32[]{:S(2)}) %collective-permute-start.7) | collective-permute-done | bytes 917536 | tf_op jit(solution)/shard_map/ppermute | solution.py:142
  95.0 4.2 %convolution_convert_fusion.1 = bf16[1024,1792]{1,0:T(8,128)(2,1)S(1)} fusion(bf16[1024,1024]{1,0:T(8,128)(2,1)S(1)} %bitcast.112, bf16[1024,1792]{1,0:T(8,128)(2,1)S(1)} %constant_dynamic-update-slice_fusion.26.refs_0_), kind=kOutput, calls=%fused_computation.3 | convolution fusion | flops 3759931392 | bytes 9437184 | tf_op jit(solution)/shard_map/dot_general | solution.py:14
  99.2 2.3 dynamic-slice_bitcast_fusion.7
  102.4 5.5 %collective-permute-start.22 = (bf16[256,1792]{1,0:T(8,128)(2,1)}, bf16[256,1792]{1,0:T(8,128)(2,1)}, u32[]{:S(2)}, u32[]{:S(2)}) collective-permute-start(bf16[256,1792]{1,0:T(8,128)(2,1)} %get-tuple-element.93), channel_id=1, source_target_pairs={{0,4},{12,8},{1,5},{13,9},{2,6},{14,10},{3,7},{15,11},{16,20},{28,... | collective-permute-start | bytes 2752520 | tf_op jit(solution)/shard_map/ppermute | solution.py:148
  108.0 3.4 %collective-permute-done.14 = bf16[512,896]{1,0:T(8,128)(2,1)} collective-permute-done((bf16[512,896]{1,0:T(8,128)(2,1)}, bf16[512,896]{1,0:T(8,128)(2,1)}, u32[]{:S(2)}, u32[]{:S(2)}) %collective-permute-start.14) | collective-permute-done | bytes 917536 | tf_op jit(solution)/shard_map/ppermute | solution.py:125
  115.3 4.2 %convolution_convert_fusion = bf16[1024,1792]{1,0:T(8,128)(2,1)S(1)} fusion(bf16[1024,1024]{1,0:T(8,128)(2,1)S(1)} %bitcast.113, bf16[1024,1792]{1,0:T(8,128)(2,1)S(1)} %constant_dynamic-update-slice_fusion.25.refs_1_), kind=kOutput, calls=%fused_computation.2 | convolution fusion | flops 3759931392 | bytes 9437184 | tf_op jit(solution)/shard_map/dot_general | solution.py:14
  120.7 2.4 dynamic-slice_bitcast_fusion.6
  123.1 5.5 %collective-permute-start.23 = (bf16[256,1792]{1,0:T(8,128)(2,1)}, bf16[256,1792]{1,0:T(8,128)(2,1)}, u32[]{:S(2)}, u32[]{:S(2)}) collective-permute-start(bf16[256,1792]{1,0:T(8,128)(2,1)} %get-tuple-element.98), channel_id=1, source_target_pairs={{0,4},{12,8},{1,5},{13,9},{2,6},{14,10},{3,7},{15,11},{16,20},{28,... | collective-permute-start | bytes 2752520 | tf_op jit(solution)/shard_map/ppermute | solution.py:148
  136.1 6.3 %collective-permute-done.23 = bf16[256,1792]{1,0:T(8,128)(2,1)} collective-permute-done((bf16[256,1792]{1,0:T(8,128)(2,1)}, bf16[256,1792]{1,0:T(8,128)(2,1)}, u32[]{:S(2)}, u32[]{:S(2)}) %collective-permute-start.23) | collective-permute-done | bytes 917536 | tf_op jit(solution)/shard_map/ppermute | solution.py:148
  145.2 1.7 maximum_add_fusion.1
  146.9 5.6 %collective-permute-start.24 = (bf16[256,3584]{1,0:T(8,128)(2,1)}, bf16[256,3584]{1,0:T(8,128)(2,1)}, u32[]{:S(2)}, u32[]{:S(2)}) collective-permute-start(bf16[256,3584]{1,0:T(8,128)(2,1)} %maximum_add_fusion.1), channel_id=1, source_target_pairs={{0,4},{4,8},{1,5},{5,9},{2,6},{6,10},{3,7},{7,11},{16,20},{20,24},... | collective-permute-start | bytes 5505032 | tf_op jit(solution)/shard_map/ppermute | solution.py:142
  152.6 1.7 maximum_add_fusion.3
  154.2 1.9 collective-permute-start.25
  156.1 2.2 constant_dynamic-update-slice_fusion.15
  162.9 9.3 %collective-permute-done.10 = bf16[256,3584]{1,0:T(8,128)(2,1)} collective-permute-done((bf16[256,3584]{1,0:T(8,128)(2,1)}, bf16[256,3584]{1,0:T(8,128)(2,1)}, u32[]{:S(2)}, u32[]{:S(2)}) %collective-permute-start.10) | collective-permute-done | bytes 1835040 | tf_op jit(solution)/shard_map/ppermute | solution.py:148
  172.1 1.7 broadcast_select_fusion.1
  176.0 1.6 collective-permute-start.29
  177.6 12.9 %shard_map.88 = bf16[1024,1024]{1,0:T(8,128)(2,1)S(1)} custom-call(bf16[1024,3584]{1,0:T(8,128)(2,1)S(1)} %get-tuple-element.64.left_ref, bf16[1024,1792]{1,0:T(8,128)(2,1)S(1)} %constant_dynamic-update-slice_fusion.26.refs_0_, bf16[1024,1792]{1,0:T(8,128)(2,1)S(1)} %constant_dynamic-update-slice_fusion.25.refs_1_), custom_call_target="tpu_custom_call" | custom-call | flops 7516192768 | bytes 29360128 | tf_op jit(solution)/shard_map/pallas_call | solution.py:46
  192.0 2.0 maximum_add_fusion
  194.1 1.9 maximum_add_fusion.2
  206.9 8.5 %multiply_convert_fusion = bf16[1024,1792]{1,0:T(8,128)(2,1)S(1)} fusion(bf16[2048,1024]{1,0:T(8,128)(2,1)S(1)} %bitcast.109, bf16[2048,1792]{1,0:T(8,128)(2,1)S(1)} %bitcast.120), kind=kOutput, calls=%fused_computation | convolution fusion | flops 7519862784 | bytes 15204352 | tf_op jit(solution)/shard_map/dot_general | solution.py:14
  215.4 3.5 %collective-permute-start.30 = (bf16[256,1792]{1,0:T(8,128)(2,1)}, bf16[256,1792]{1,0:T(8,128)(2,1)}, u32[]{:S(2)}, u32[]{:S(2)}) collective-permute-start(bf16[256,1792]{1,0:T(8,128)(2,1)} %get-tuple-element.69), channel_id=1, source_target_pairs={{0,4},{4,8},{8,12},{1,5},{5,9},{9,13},{2,6},{6,10},{10,14},{3,7},{... | collective-permute-start | bytes 2752520 | tf_op jit(solution)/shard_map/ppermute | solution.py:142
  220.2 1.6 dynamic-slice_bitcast_fusion.1
  221.8 1.7 collective-permute-start.37
  227.2 9.8 %collective-permute-done.30 = bf16[256,1792]{1,0:T(8,128)(2,1)} collective-permute-done((bf16[256,1792]{1,0:T(8,128)(2,1)}, bf16[256,1792]{1,0:T(8,128)(2,1)}, u32[]{:S(2)}, u32[]{:S(2)}) %collective-permute-start.30) | collective-permute-done | bytes 917536 | tf_op jit(solution)/shard_map/ppermute | solution.py:142
  237.0 5.0 %collective-permute-done.31 = bf16[256,1792]{1,0:T(8,128)(2,1)} collective-permute-done((bf16[256,1792]{1,0:T(8,128)(2,1)}, bf16[256,1792]{1,0:T(8,128)(2,1)}, u32[]{:S(2)}, u32[]{:S(2)}) %collective-permute-start.31) | collective-permute-done | bytes 917536 | tf_op jit(solution)/shard_map/ppermute | solution.py:142
  242.1 2.9 %collective-permute-start.32 = (bf16[256,1792]{1,0:T(8,128)(2,1)S(1)}, bf16[256,1792]{1,0:T(8,128)(2,1)S(1)}, u32[]{:S(2)}, u32[]{:S(2)}) collective-permute-start(bf16[256,1792]{1,0:T(8,128)(2,1)S(1)} %get-tuple-element.71), channel_id=1, source_target_pairs={{0,4},{4,8},{8,12},{1,5},{5,9},{9,13},{2,6},{6,10},{10,14},{3,7},{... | collective-permute-start | bytes 2752520 | tf_op jit(solution)/shard_map/ppermute | solution.py:142
  247.1 2.1 add_convert_fusion.1
  253.4 10.5 %collective-permute-done.39 = bf16[256,1792]{1,0:T(8,128)(2,1)S(1)} collective-permute-done((bf16[256,1792]{1,0:T(8,128)(2,1)}, bf16[256,1792]{1,0:T(8,128)(2,1)S(1)}, u32[]{:S(2)}, u32[]{:S(2)}) %collective-permute-start.39) | collective-permute-done | bytes 917536 | tf_op jit(solution)/shard_map/ppermute | solution.py:133
  264.6 2.6 collective-permute-done.33
  267.3 2.3 collective-permute-start.34
  272.2 1.8 collective-permute-start.41
  275.7 3.6 %collective-permute-done.35 = bf16[64,1024]{1,0:T(8,128)(2,1)S(1)} collective-permute-done((bf16[64,1024]{1,0:T(8,128)(2,1)S(1)}, bf16[64,1024]{1,0:T(8,128)(2,1)S(1)}, u32[]{:S(2)}, u32[]{:S(2)}) %collective-permute-start.35) | collective-permute-done | bytes 131104 | tf_op jit(solution)/shard_map/ppermute | solution.py:125
  279.4 4.1 %collective-permute-done.41 = bf16[128,1792]{1,0:T(8,128)(2,1)S(1)} collective-permute-done((bf16[128,1792]{1,0:T(8,128)(2,1)S(1)}, bf16[128,1792]{1,0:T(8,128)(2,1)S(1)}, u32[]{:S(2)}, u32[]{:S(2)}) %collective-permute-start.41) | collective-permute-done | bytes 458784 | tf_op jit(solution)/shard_map/ppermute | solution.py:125
  (204 shorter events, 81.1 us)
Async XLA Ops:
  5.0 38.9 %collective-permute-start = (bf16[128,3584]{1,0:T(8,128)(2,1)}, bf16[128,3584]{1,0:T(8,128)(2,1)S(1)}, u32[]{:S(2)}, u32[]{:S(2)}) collective-permute-start(bf16[128,3584]{1,0:T(8,128)(2,1)} %pad_maximum_fusion.8), channel_id=1, source_target_pairs={{0,2},{2,0},{1,3},{3,1},{4,6},{6,4},{5,7},{7,5},{8,10},{10,8},{9,1... | collective-permute-start | bytes 2752520 | tf_op jit(solution)/shard_map/ppermute | solution.py:125
  9.3 27.4 %collective-permute-start.3 = (bf16[64,2048]{1,0:T(8,128)(2,1)S(1)}, bf16[64,2048]{1,0:T(8,128)(2,1)}, u32[]{:S(2)}, u32[]{:S(2)}) collective-permute-start(bf16[64,2048]{1,0:T(8,128)(2,1)S(1)} %pad_maximum_fusion.20), channel_id=1, source_target_pairs={{0,12},{4,0},{8,4},{12,8},{1,13},{5,1},{9,5},{13,9},{2,14},{6,2},{... | collective-permute-start | bytes 786440 | tf_op jit(solution)/shard_map/ppermute | solution.py:125
  13.0 23.7 %collective-permute-start.2 = (bf16[64,2048]{1,0:T(8,128)(2,1)S(1)}, bf16[64,2048]{1,0:T(8,128)(2,1)}, u32[]{:S(2)}, u32[]{:S(2)}) collective-permute-start(bf16[64,2048]{1,0:T(8,128)(2,1)S(1)} %pad_maximum_fusion.19), channel_id=1, source_target_pairs={{0,8},{4,12},{8,0},{12,4},{1,9},{5,13},{9,1},{13,5},{2,10},{6,14},... | collective-permute-start | bytes 786440 | tf_op jit(solution)/shard_map/ppermute | solution.py:125
  13.8 23.0 %collective-permute-start.1 = (bf16[64,2048]{1,0:T(8,128)(2,1)}, bf16[64,2048]{1,0:T(8,128)(2,1)}, u32[]{:S(2)}, u32[]{:S(2)}) collective-permute-start(bf16[64,2048]{1,0:T(8,128)(2,1)} %pad_maximum_fusion.18), channel_id=1, source_target_pairs={{0,4},{4,8},{8,12},{12,0},{1,5},{5,9},{9,13},{13,1},{2,6},{6,10},{... | collective-permute-start | bytes 786440 | tf_op jit(solution)/shard_map/ppermute | solution.py:125
  20.1 28.2 %collective-permute-start.11 = (bf16[512,896]{1,0:T(8,128)(2,1)}, bf16[512,896]{1,0:T(8,128)(2,1)S(1)}, u32[]{:S(2)}, u32[]{:S(2)}) collective-permute-start(bf16[512,896]{1,0:T(8,128)(2,1)} %shard_map.84), channel_id=1, source_target_pairs={{0,2},{2,0},{1,3},{3,1},{4,6},{6,4},{5,7},{7,5},{8,10},{10,8},{9,1... | collective-permute-start | bytes 2752520 | tf_op jit(solution)/shard_map/ppermute | solution.py:125
  38.1 22.9 %collective-permute-start.4 = (bf16[128,3584]{1,0:T(8,128)(2,1)S(1)}, bf16[128,3584]{1,0:T(8,128)(2,1)S(1)}, u32[]{:S(2)}, u32[]{:S(2)}) collective-permute-start(bf16[128,3584]{1,0:T(8,128)(2,1)S(1)} %copy-done.20), channel_id=1, source_target_pairs={{0,4},{4,8},{8,12},{1,5},{5,9},{9,13},{2,6},{6,10},{10,14},{3,7},{... | collective-permute-start | bytes 2752520 | tf_op jit(solution)/shard_map/ppermute | solution.py:142
  42.6 22.6 %collective-permute-start.5 = (bf16[128,3584]{1,0:T(8,128)(2,1)S(1)}, bf16[128,3584]{1,0:T(8,128)(2,1)S(1)}, u32[]{:S(2)}, u32[]{:S(2)}) collective-permute-start(bf16[128,3584]{1,0:T(8,128)(2,1)S(1)} %copy-done.20), channel_id=1, source_target_pairs={{12,8},{8,4},{4,0},{13,9},{9,5},{5,1},{14,10},{10,6},{6,2},{15,11}... | collective-permute-start | bytes 2752520 | tf_op jit(solution)/shard_map/ppermute | solution.py:142
  44.0 7.5 %copy-start.1 = (bf16[1024,1792]{1,0:T(8,128)(2,1)S(1)}, bf16[1024,1792]{1,0:T(8,128)(2,1)}, u32[]{:S(2)}) copy-start(bf16[1024,1792]{1,0:T(8,128)(2,1)} %shard_map.85) | copy-start | bytes 11010052
  48.2 22.4 %collective-permute-start.16 = (bf16[512,896]{1,0:T(8,128)(2,1)S(1)}, bf16[512,896]{1,0:T(8,128)(2,1)S(1)}, u32[]{:S(2)}, u32[]{:S(2)}) collective-permute-start(bf16[512,896]{1,0:T(8,128)(2,1)S(1)} %collective-permute-done.11), channel_id=1, source_target_pairs={{0,16},{16,0},{1,17},{17,1},{2,18},{18,2},{3,19},{19,3},{4,20},{20... | collective-permute-start | bytes 2752520 | tf_op jit(solution)/shard_map/ppermute | solution.py:125
  49.9 18.9 %collective-permute-start.12 = (bf16[4,64,1024]{2,1,0:T(8,128)(2,1)S(1)}, bf16[4,64,1024]{2,1,0:T(8,128)(2,1)S(1)}, u32[]{:S(2)}, u32[]{:S(2)}) collective-permute-start(bf16[4,64,1024]{2,1,0:T(8,128)(2,1)S(1)} %get-tuple-element.57), channel_id=1, source_target_pairs={{0,2},{2,0},{1,3},{3,1},{4,6},{6,4},{5,7},{7,5},{8,10},{10,8},{9,1... | collective-permute-start | bytes 1572872 | tf_op jit(solution)/shard_map/ppermute | solution.py:125
  52.6 16.2 %copy-start.19 = (bf16[512,896]{1,0:T(8,128)(2,1)S(1)}, bf16[512,896]{1,0:T(8,128)(2,1)}, u32[]{:S(2)}) copy-start(bf16[512,896]{1,0:T(8,128)(2,1)} %shard_map.87) | copy-start | bytes 2752516
  65.2 19.7 %collective-permute-start.6 = (bf16[128,3584]{1,0:T(8,128)(2,1)S(1)}, bf16[128,3584]{1,0:T(8,128)(2,1)S(1)}, u32[]{:S(2)}, u32[]{:S(2)}) collective-permute-start(bf16[128,3584]{1,0:T(8,128)(2,1)S(1)} %collective-permute-done), channel_id=1, source_target_pairs={{0,4},{4,8},{8,12},{1,5},{5,9},{9,13},{2,6},{6,10},{10,14},{3,7},{... | collective-permute-start | bytes 2752520 | tf_op jit(solution)/shard_map/ppermute | solution.py:142
  67.4 21.7 %collective-permute-start.7 = (bf16[128,3584]{1,0:T(8,128)(2,1)S(1)}, bf16[128,3584]{1,0:T(8,128)(2,1)S(1)}, u32[]{:S(2)}, u32[]{:S(2)}) collective-permute-start(bf16[128,3584]{1,0:T(8,128)(2,1)S(1)} %collective-permute-done), channel_id=1, source_target_pairs={{12,8},{8,4},{4,0},{13,9},{9,5},{5,1},{14,10},{10,6},{6,2},{15,11}... | collective-permute-start | bytes 2752520 | tf_op jit(solution)/shard_map/ppermute | solution.py:142
  68.7 21.7 %slice-start = ((s8[7340032]{0:T(1024)(128)(4,1)}), s8[4194304]{0:T(1024)(128)(4,1)S(1)}, s32[]{:S(2)}) async-start(s8[7340032]{0:T(1024)(128)(4,1)} %bitcast.103), calls=%async_computation | async-start | bytes 8388608
  68.8 23.2 %collective-permute-start.13 = (bf16[512,896]{1,0:T(8,128)(2,1)S(1)}, bf16[512,896]{1,0:T(8,128)(2,1)}, u32[]{:S(2)}, u32[]{:S(2)}) collective-permute-start(bf16[512,896]{1,0:T(8,128)(2,1)S(1)} %copy-done.19), channel_id=1, source_target_pairs={{0,2},{2,0},{1,3},{3,1},{4,6},{6,4},{5,7},{7,5},{8,10},{10,8},{9,1... | collective-permute-start | bytes 2752520 | tf_op jit(solution)/shard_map/ppermute | solution.py:125
  70.2 24.7 %collective-permute-start.15 = (bf16[4,2,64,1024]{3,2,1,0:T(8,128)(2,1)S(1)}, bf16[4,2,64,1024]{3,2,1,0:T(8,128)(2,1)S(1)}, u32[]{:S(2)}, u32[]{:S(2)}) collective-permute-start(bf16[4,2,64,1024]{3,2,1,0:T(8,128)(2,1)S(1)} %pad_maximum_fusion.6), channel_id=1, source_target_pairs={{0,1},{1,0},{2,3},{3,2},{4,5},{5,4},{6,7},{7,6},{8,9},{9,8},{10,11... | collective-permute-start | bytes 3145736 | tf_op jit(solution)/shard_map/ppermute | solution.py:125
  70.5 19.9 %slice-start.1 = ((s8[7340032]{0:T(1024)(128)(4,1)}), s8[3145728]{0:T(1024)(128)(4,1)S(1)}, s32[]{:S(2)}) async-start(s8[7340032]{0:T(1024)(128)(4,1)} %bitcast.103), calls=%async_computation.1 | async-start | bytes 6291456
  70.7 20.2 %collective-permute-start.26 = (bf16[4,64,1024]{2,1,0:T(8,128)(2,1)S(1)}, bf16[4,64,1024]{2,1,0:T(8,128)(2,1)S(1)}, u32[]{:S(2)}, u32[]{:S(2)}) collective-permute-start(bf16[4,64,1024]{2,1,0:T(8,128)(2,1)S(1)} %get-tuple-element.67), channel_id=1, source_target_pairs={{0,16},{16,0},{1,17},{17,1},{2,18},{18,2},{3,19},{19,3},{4,20},{20... | collective-permute-start | bytes 1572872 | tf_op jit(solution)/shard_map/ppermute | solution.py:125
  84.9 45.2 %collective-permute-start.8 = (bf16[256,3584]{1,0:T(8,128)(2,1)S(1)}, bf16[256,3584]{1,0:T(8,128)(2,1)S(1)}, u32[]{:S(2)}, u32[]{:S(2)}) collective-permute-start(bf16[256,3584]{1,0:T(8,128)(2,1)S(1)} %constant_dynamic-update-slice_fusion), channel_id=1, source_target_pairs={{4,8},{8,12},{5,9},{9,13},{6,10},{10,14},{7,11},{11,15},{20,24},{2... | collective-permute-start | bytes 5505032 | tf_op jit(solution)/shard_map/ppermute | solution.py:142
  89.1 41.0 %collective-permute-start.9 = (bf16[256,3584]{1,0:T(8,128)(2,1)S(1)}, bf16[256,3584]{1,0:T(8,128)(2,1)S(1)}, u32[]{:S(2)}, u32[]{:S(2)}) collective-permute-start(bf16[256,3584]{1,0:T(8,128)(2,1)S(1)} %constant_dynamic-update-slice_fusion.2), channel_id=1, source_target_pairs={{8,4},{4,0},{9,5},{5,1},{10,6},{6,2},{11,7},{7,3},{24,20},{20,16},... | collective-permute-start | bytes 5505032 | tf_op jit(solution)/shard_map/ppermute | solution.py:142
  91.1 32.1 %collective-permute-start.27 = (bf16[4,2,64,1024]{3,2,0,1:T(8,128)(2,1)S(1)}, bf16[4,2,64,1024]{3,2,0,1:T(8,128)(2,1)S(1)}, u32[]{:S(2)}, u32[]{:S(2)}) collective-permute-start(bf16[4,2,64,1024]{3,2,0,1:T(8,128)(2,1)S(1)} %get-tuple-element.146), channel_id=1, source_target_pairs={{0,2},{2,0},{1,3},{3,1},{4,6},{6,4},{5,7},{7,5},{8,10},{10,8},{9,1... | collective-permute-start | bytes 3145736 | tf_op jit(solution)/shard_map/ppermute | solution.py:125
  92.0 19.4 %collective-permute-start.14 = (bf16[512,896]{1,0:T(8,128)(2,1)}, bf16[512,896]{1,0:T(8,128)(2,1)}, u32[]{:S(2)}, u32[]{:S(2)}) collective-permute-start(bf16[512,896]{1,0:T(8,128)(2,1)} %collective-permute-done.13), channel_id=1, source_target_pairs={{0,16},{16,0},{1,17},{17,1},{2,18},{18,2},{3,19},{19,3},{4,20},{20... | collective-permute-start | bytes 2752520 | tf_op jit(solution)/shard_map/ppermute | solution.py:125
  102.4 26.4 %collective-permute-start.22 = (bf16[256,1792]{1,0:T(8,128)(2,1)}, bf16[256,1792]{1,0:T(8,128)(2,1)}, u32[]{:S(2)}, u32[]{:S(2)}) collective-permute-start(bf16[256,1792]{1,0:T(8,128)(2,1)} %get-tuple-element.93), channel_id=1, source_target_pairs={{0,4},{12,8},{1,5},{13,9},{2,6},{14,10},{3,7},{15,11},{16,20},{28,... | collective-permute-start | bytes 2752520 | tf_op jit(solution)/shard_map/ppermute | solution.py:148
  112.5 21.2 %collective-permute-start.17 = (bf16[256,1792]{1,0:T(8,128)(2,1)}, bf16[256,1792]{1,0:T(8,128)(2,1)}, u32[]{:S(2)}, u32[]{:S(2)}) collective-permute-start(bf16[256,1792]{1,0:T(8,128)(2,1)} %pad_maximum_fusion.11), channel_id=1, source_target_pairs={{0,16},{16,0},{1,17},{17,1},{2,18},{18,2},{3,19},{19,3},{4,20},{20... | collective-permute-start | bytes 2752520 | tf_op jit(solution)/shard_map/ppermute | solution.py:125
  123.1 19.3 %collective-permute-start.23 = (bf16[256,1792]{1,0:T(8,128)(2,1)}, bf16[256,1792]{1,0:T(8,128)(2,1)}, u32[]{:S(2)}, u32[]{:S(2)}) collective-permute-start(bf16[256,1792]{1,0:T(8,128)(2,1)} %get-tuple-element.98), channel_id=1, source_target_pairs={{0,4},{12,8},{1,5},{13,9},{2,6},{14,10},{3,7},{15,11},{16,20},{28,... | collective-permute-start | bytes 2752520 | tf_op jit(solution)/shard_map/ppermute | solution.py:148
  132.5 39.7 %collective-permute-start.10 = (bf16[256,3584]{1,0:T(8,128)(2,1)}, bf16[256,3584]{1,0:T(8,128)(2,1)}, u32[]{:S(2)}, u32[]{:S(2)}) collective-permute-start(bf16[256,3584]{1,0:T(8,128)(2,1)} %broadcast_select_fusion), channel_id=1, source_target_pairs={{8,12},{4,0},{9,13},{5,1},{10,14},{6,2},{11,15},{7,3},{24,28},{20,... | collective-permute-start | bytes 5505032 | tf_op jit(solution)/shard_map/ppermute | solution.py:148
  135.0 24.3 %collective-permute-start.18 = (bf16[256,1792]{1,0:T(8,128)(2,1)}, bf16[256,1792]{1,0:T(8,128)(2,1)S(1)}, u32[]{:S(2)}, u32[]{:S(2)}) collective-permute-start(bf16[256,1792]{1,0:T(8,128)(2,1)} %pad_maximum_fusion.13), channel_id=1, source_target_pairs={{0,16},{16,0},{1,17},{17,1},{2,18},{18,2},{3,19},{19,3},{4,20},{20... | collective-permute-start | bytes 2752520 | tf_op jit(solution)/shard_map/ppermute | solution.py:125
  145.2 7.4 %copy-start.14 = (bf16[256,1792]{1,0:T(8,128)(2,1)S(1)}, bf16[256,1792]{1,0:T(8,128)(2,1)}, u32[]{:S(2)}) copy-start(bf16[256,1792]{1,0:T(8,128)(2,1)} %get-tuple-element.97) | copy-start | bytes 2752516
  146.9 44.0 %collective-permute-start.24 = (bf16[256,3584]{1,0:T(8,128)(2,1)}, bf16[256,3584]{1,0:T(8,128)(2,1)}, u32[]{:S(2)}, u32[]{:S(2)}) collective-permute-start(bf16[256,3584]{1,0:T(8,128)(2,1)} %maximum_add_fusion.1), channel_id=1, source_target_pairs={{0,4},{4,8},{1,5},{5,9},{2,6},{6,10},{3,7},{7,11},{16,20},{20,24},... | collective-permute-start | bytes 5505032 | tf_op jit(solution)/shard_map/ppermute | solution.py:142
  154.2 39.8 %collective-permute-start.25 = (bf16[256,3584]{1,0:T(8,128)(2,1)}, bf16[256,3584]{1,0:T(8,128)(2,1)}, u32[]{:S(2)}, u32[]{:S(2)}) collective-permute-start(bf16[256,3584]{1,0:T(8,128)(2,1)} %maximum_add_fusion.3), channel_id=1, source_target_pairs={{12,8},{8,4},{13,9},{9,5},{14,10},{10,6},{15,11},{11,7},{28,24},{2... | collective-permute-start | bytes 5505032 | tf_op jit(solution)/shard_map/ppermute | solution.py:142
  159.6 16.2 %collective-permute-start.19 = (bf16[256,1792]{1,0:T(8,128)(2,1)S(1)}, bf16[256,1792]{1,0:T(8,128)(2,1)S(1)}, u32[]{:S(2)}, u32[]{:S(2)}) collective-permute-start(bf16[256,1792]{1,0:T(8,128)(2,1)S(1)} %pad_maximum_fusion.15), channel_id=1, source_target_pairs={{0,16},{16,0},{1,17},{17,1},{2,18},{18,2},{3,19},{19,3},{4,20},{20... | collective-permute-start | bytes 2752520 | tf_op jit(solution)/shard_map/ppermute | solution.py:125
  173.9 28.8 %collective-permute-start.28 = (bf16[4,2,2,64,1024]{4,3,0,1,2:T(8,128)(2,1)S(1)}, bf16[4,2,2,64,1024]{4,3,0,1,2:T(8,128)(2,1)S(1)}, u32[]{:S(2)}, u32[]{:S(2)}) collective-permute-start(bf16[4,2,2,64,1024]{4,3,0,1,2:T(8,128)(2,1)S(1)} %pad_maximum_fusion.1), channel_id=1, source_target_pairs={{0,1},{1,0},{2,3},{3,2},{4,5},{5,4},{6,7},{7,6},{8,9},{9,8},{10,11... | collective-permute-start | bytes 6291464 | tf_op jit(solution)/shard_map/ppermute | solution.py:125
  176.0 24.1 %collective-permute-start.29 = (bf16[256,1792]{1,0:T(8,128)(2,1)S(1)}, bf16[256,1792]{1,0:T(8,128)(2,1)S(1)}, u32[]{:S(2)}, u32[]{:S(2)}) collective-permute-start(bf16[256,1792]{1,0:T(8,128)(2,1)S(1)} %pad_maximum_fusion.17), channel_id=1, source_target_pairs={{0,16},{16,0},{1,17},{17,1},{2,18},{18,2},{3,19},{19,3},{4,20},{20... | collective-permute-start | bytes 2752520 | tf_op jit(solution)/shard_map/ppermute | solution.py:125
  190.6 10.5 %collective-permute-start.20 = (bf16[4,2,64,1024]{3,2,1,0:T(8,128)(2,1)S(1)}, bf16[4,2,64,1024]{3,2,1,0:T(8,128)(2,1)S(1)}, u32[]{:S(2)}, u32[]{:S(2)}) collective-permute-start(bf16[4,2,64,1024]{3,2,1,0:T(8,128)(2,1)S(1)} %dynamic-slice_bitcast_fusion), channel_id=1, source_target_pairs={{0,1},{1,0},{2,3},{3,2},{4,5},{5,4},{6,7},{7,6},{8,9},{9,8},{10,11... | collective-permute-start | bytes 3145736 | tf_op jit(solution)/shard_map/ppermute | solution.py:125
  202.4 21.6 %collective-permute-start.21 = (bf16[4,64,1024]{2,1,0:T(8,128)(2,1)}, bf16[4,64,1024]{2,1,0:T(8,128)(2,1)S(1)}, u32[]{:S(2)}, u32[]{:S(2)}) collective-permute-start(bf16[4,64,1024]{2,1,0:T(8,128)(2,1)} %slice_bitcast_fusion), channel_id=1, source_target_pairs={{0,2},{2,0},{1,3},{3,1},{4,6},{6,4},{5,7},{7,5},{8,10},{10,8},{9,1... | collective-permute-start | bytes 1572872 | tf_op jit(solution)/shard_map/ppermute | solution.py:125
  215.4 21.6 %collective-permute-start.30 = (bf16[256,1792]{1,0:T(8,128)(2,1)}, bf16[256,1792]{1,0:T(8,128)(2,1)}, u32[]{:S(2)}, u32[]{:S(2)}) collective-permute-start(bf16[256,1792]{1,0:T(8,128)(2,1)} %get-tuple-element.69), channel_id=1, source_target_pairs={{0,4},{4,8},{8,12},{1,5},{5,9},{9,13},{2,6},{6,10},{10,14},{3,7},{... | collective-permute-start | bytes 2752520 | tf_op jit(solution)/shard_map/ppermute | solution.py:142
  218.9 23.2 %collective-permute-start.31 = (bf16[256,1792]{1,0:T(8,128)(2,1)}, bf16[256,1792]{1,0:T(8,128)(2,1)}, u32[]{:S(2)}, u32[]{:S(2)}) collective-permute-start(bf16[256,1792]{1,0:T(8,128)(2,1)} %get-tuple-element.70), channel_id=1, source_target_pairs={{12,8},{8,4},{4,0},{13,9},{9,5},{5,1},{14,10},{10,6},{6,2},{15,11}... | collective-permute-start | bytes 2752520 | tf_op jit(solution)/shard_map/ppermute | solution.py:142
  221.8 24.7 %collective-permute-start.37 = (bf16[256,1792]{1,0:T(8,128)(2,1)}, bf16[256,1792]{1,0:T(8,128)(2,1)}, u32[]{:S(2)}, u32[]{:S(2)}) collective-permute-start(bf16[256,1792]{1,0:T(8,128)(2,1)} %get-tuple-element.90), channel_id=1, source_target_pairs={{0,2},{2,0},{16,18},{18,16},{1,3},{3,1},{17,19},{19,17},{4,6},{6,4... | collective-permute-start | bytes 2752520 | tf_op jit(solution)/shard_map/ppermute | solution.py:133
  223.4 23.6 %collective-permute-start.38 = (bf16[256,1792]{1,0:T(8,128)(2,1)}, bf16[256,1792]{1,0:T(8,128)(2,1)}, u32[]{:S(2)}, u32[]{:S(2)}) collective-permute-start(bf16[256,1792]{1,0:T(8,128)(2,1)} %get-tuple-element.89), channel_id=1, source_target_pairs={{0,16},{2,18},{16,0},{18,2},{1,17},{3,19},{17,1},{19,3},{4,20},{6,... | collective-permute-start | bytes 2752520 | tf_op jit(solution)/shard_map/ppermute | solution.py:133
  224.2 39.8 %collective-permute-start.39 = (bf16[256,1792]{1,0:T(8,128)(2,1)}, bf16[256,1792]{1,0:T(8,128)(2,1)S(1)}, u32[]{:S(2)}, u32[]{:S(2)}) collective-permute-start(bf16[256,1792]{1,0:T(8,128)(2,1)} %get-tuple-element.88), channel_id=1, source_target_pairs={{0,18},{2,16},{16,2},{18,0},{1,19},{3,17},{17,3},{19,1},{4,22},{6,... | collective-permute-start | bytes 2752520 | tf_op jit(solution)/shard_map/ppermute | solution.py:133
  242.1 22.6 %collective-permute-start.32 = (bf16[256,1792]{1,0:T(8,128)(2,1)S(1)}, bf16[256,1792]{1,0:T(8,128)(2,1)S(1)}, u32[]{:S(2)}, u32[]{:S(2)}) collective-permute-start(bf16[256,1792]{1,0:T(8,128)(2,1)S(1)} %get-tuple-element.71), channel_id=1, source_target_pairs={{0,4},{4,8},{8,12},{1,5},{5,9},{9,13},{2,6},{6,10},{10,14},{3,7},{... | collective-permute-start | bytes 2752520 | tf_op jit(solution)/shard_map/ppermute | solution.py:142
  244.9 22.3 %collective-permute-start.33 = (bf16[256,1792]{1,0:T(8,128)(2,1)S(1)}, bf16[256,1792]{1,0:T(8,128)(2,1)S(1)}, u32[]{:S(2)}, u32[]{:S(2)}) collective-permute-start(bf16[256,1792]{1,0:T(8,128)(2,1)S(1)} %get-tuple-element.72), channel_id=1, source_target_pairs={{12,8},{8,4},{4,0},{13,9},{9,5},{5,1},{14,10},{10,6},{6,2},{15,11}... | collective-permute-start | bytes 2752520 | tf_op jit(solution)/shard_map/ppermute | solution.py:142
  249.2 25.7 %collective-permute-start.40 = (bf16[128,1792]{1,0:T(8,128)(2,1)S(1)}, bf16[128,1792]{1,0:T(8,128)(2,1)S(1)}, u32[]{:S(2)}, u32[]{:S(2)}) collective-permute-start(bf16[128,1792]{1,0:T(8,128)(2,1)S(1)} %slice.162), channel_id=1, source_target_pairs={{0,2},{2,0},{1,3},{3,1},{4,6},{6,4},{5,7},{7,5},{8,10},{10,8},{9,1... | collective-permute-start | bytes 1376264 | tf_op jit(solution)/shard_map/ppermute | solution.py:125
  253.4 10.8 %copy-start.5 = (bf16[128,7168]{1,0:T(8,128)(2,1)S(1)}, bf16[128,7168]{1,0:T(8,128)(2,1)}, u32[]{:S(2)}) copy-start(bf16[128,7168]{1,0:T(8,128)(2,1)} %param.6) | copy-start | bytes 5505028
  267.3 8.4 %collective-permute-start.34 = (bf16[64,1024]{1,0:T(8,128)(2,1)S(1)}, bf16[64,1024]{1,0:T(8,128)(2,1)S(1)}, u32[]{:S(2)}, u32[]{:S(2)}) collective-permute-start(bf16[64,1024]{1,0:T(8,128)(2,1)S(1)} %get-tuple-element.173), channel_id=1, source_target_pairs={{0,12},{4,0},{8,4},{12,8},{1,13},{5,1},{9,5},{13,9},{2,14},{6,2},{... | collective-permute-start | bytes 393224 | tf_op jit(solution)/shard_map/ppermute | solution.py:125
  269.6 9.7 %collective-permute-start.35 = (bf16[64,1024]{1,0:T(8,128)(2,1)S(1)}, bf16[64,1024]{1,0:T(8,128)(2,1)S(1)}, u32[]{:S(2)}, u32[]{:S(2)}) collective-permute-start(bf16[64,1024]{1,0:T(8,128)(2,1)S(1)} %get-tuple-element.172), channel_id=1, source_target_pairs={{0,8},{4,12},{8,0},{12,4},{1,9},{5,13},{9,1},{13,5},{2,10},{6,14},... | collective-permute-start | bytes 393224 | tf_op jit(solution)/shard_map/ppermute | solution.py:125
  269.7 9.6 %collective-permute-start.36 = (bf16[64,1024]{1,0:T(8,128)(2,1)S(1)}, bf16[64,1024]{1,0:T(8,128)(2,1)S(1)}, u32[]{:S(2)}, u32[]{:S(2)}) collective-permute-start(bf16[64,1024]{1,0:T(8,128)(2,1)S(1)} %get-tuple-element.171), channel_id=1, source_target_pairs={{0,4},{4,8},{8,12},{12,0},{1,5},{5,9},{9,13},{13,1},{2,6},{6,10},{... | collective-permute-start | bytes 393224 | tf_op jit(solution)/shard_map/ppermute | solution.py:125
  272.2 11.2 %collective-permute-start.41 = (bf16[128,1792]{1,0:T(8,128)(2,1)S(1)}, bf16[128,1792]{1,0:T(8,128)(2,1)S(1)}, u32[]{:S(2)}, u32[]{:S(2)}) collective-permute-start(bf16[128,1792]{1,0:T(8,128)(2,1)S(1)} %slice.165), channel_id=1, source_target_pairs={{0,2},{2,0},{1,3},{3,1},{4,6},{6,4},{5,7},{7,5},{8,10},{10,8},{9,1... | collective-permute-start | bytes 1376264 | tf_op jit(solution)/shard_map/ppermute | solution.py:125
  (22 other events, 67.5 us)
where the time goes:
time: 287 us; the launch traced here: 286 us
  waiting for transfers between devices  87.8 us (31%)
  starting transfers between devices  73.2 us (26%)
  other arithmetic  40.8 us (14%)
  local copies, waits for them, and re-layouts  36.8 us (13%)
  Pallas kernels  28.9 us (10%)
  matrix products  16.9 us (6%)
    ppermute x6, waiting for transfers between devices, send_lines(): lax.ppermute(up_value, 'z', ups)  30.7 us
    ppermute x24, starting transfers between devices, send_ring(): lax.ppermute(value, axis, [(i, (i + shift) % size) for i in range(size)])  29.3 us
    ppermute x6, starting transfers between devices, send_lines(): lax.ppermute(up_value, 'z', ups)  19.4 us
    dot_general x3, matrix products, contract(): lax.dot_general(left, right, (((left_dim,), (right_dim,)), ((), ())), pre...  16.9 us
    pallas_call x4, Pallas kernels, dequantize_pieces(): pl.pallas_call(functools.partial(scale_body, block), out_shape=jax.ShapeD...  16 us
    ppermute x3, waiting for transfers between devices, send_lines(): lax.ppermute(jnp.where(is_up, up_value, down_value), 'z', ups + downs)  15.6 us
    ppermute x24, waiting for transfers between devices, send_ring(): lax.ppermute(value, axis, [(i, (i + shift) % size) for i in range(size)])  15.3 us
    ppermute x6, waiting for transfers between devices, send_lines(): lax.ppermute(down_value, 'z', downs)  15.2 us
  transfers between devices with their start and end apart: 42, of which 15 were waited for; matrix products, arithmetic and copies ran while one was open for 29% of the time, Pallas kernels for 10%

commit v1 on v0

--- a/solution.py
+++ b/solution.py
@@ -82,7 +82,7 @@
         return lax.dynamic_update_slice_in_dim(
             jnp.zeros((slots * rows, parts.shape[1]), jnp.bfloat16), parts, slot * rows, 0
         )
-    count, tile = len(indices), 256
+    count, tile = len(indices), 512 if rows % 512 == 0 else 256
     return pl.pallas_call(
         functools.partial(scale_body, block),
         out_shape=jax.ShapeDtypeStruct((slots * rows, count * piece), jnp.bfloat16),
@@ -207,6 +207,7 @@
     along = [plane_features(z)]
     for shift in range(1, depth):
         along.append(send_ring(plane_features(lax.rem(z + shift, depth)), "z", depth, shift))
+    nearby = along[1]
     along = jnp.stack(along)
 
     def weight_parts(places, h, codes, *slots):
@@ -214,8 +215,8 @@
         return dequantize_pieces(codes, scales, indices, piece, *slots)
 
     given = [[weight_parts([(0, dy)], h, weight_codes) for dy in range(1, pairs)] for h in range(halves)]
-    own = [weight_parts([(dx, 0) for dx in range(copies)], h, after(weight_codes, given[0][0]), pairs, y) for h in range(halves)]
-    early = send_lines(*(after(groups[0], along),) * 2, range(depth - 1))
+    own = [weight_parts([(dx, 0) for dx in range(copies)], h, after(weight_codes, given[0][0], nearby), pairs, y) for h in range(halves)]
+    early = send_lines(*(after(groups[0], nearby),) * 2, range(depth - 1))
     groups = [groups[0]] + after(groups[1:], *own, *given[1])
     steps = [(jnp.concatenate(groups, axis=0),) * 2]
 

time: 287 us -> 279 us (0.972)
  waiting for transfers between devices: 87.8 us -> 78.7 us
    ppermute x6, waiting for transfers between devices: 30.7 us -> 16.1 us  [send_lines(): lax.ppermute(up_value, 'z', ups)]
    ppermute x3, waiting for transfers between devices: 15.6 us -> 9.8 us  [send_lines(): lax.ppermute(jnp.where(is_up, up_value, down_value), 'z', ups + downs)]
    ppermute x24, waiting for transfers between devices: 15.3 us -> 20.1 us  [send_ring(): lax.ppermute(value, axis, [(i, (i + shift) % size) for i in range(size)])]
    ppermute x6, waiting for transfers between devices: 15.2 us -> 19.6 us  [send_lines(): lax.ppermute(down_value, 'z', downs)]
  transfers between devices with their start and end apart: 42 -> 42, of which waited for: 15 -> 16; matrix products, arithmetic and copies ran while one was open for 29% -> 30% of each run, Pallas kernels for 10% -> 10%
where the time goes in v1:
time: 279 us; the launch traced here: 277 us
  waiting for transfers between devices  78.7 us (28%)
  starting transfers between devices  74.3 us (27%)
  other arithmetic  40.1 us (14%)
  local copies, waits for them, and re-layouts  38.8 us (14%)
  Pallas kernels  26.8 us (10%)
  matrix products  16.9 us (6%)
    ppermute x24, starting transfers between devices, send_ring(): lax.ppermute(value, axis, [(i, (i + shift) % size) for i in range(size)])  28.7 us
    ppermute x6, starting transfers between devices, send_lines(): lax.ppermute(up_value, 'z', ups)  21.1 us
    ppermute x24, waiting for transfers between devices, send_ring(): lax.ppermute(value, axis, [(i, (i + shift) % size) for i in range(size)])  20.1 us
    ppermute x6, waiting for transfers between devices, send_lines(): lax.ppermute(down_value, 'z', downs)  19.6 us
    dot_general x3, matrix products, contract(): lax.dot_general(left, right, (((left_dim,), (right_dim,)), ((), ())), pre...  16.9 us
    ppermute x6, waiting for transfers between devices, send_lines(): lax.ppermute(up_value, 'z', ups)  16.1 us
    unnamed x63, local copies, waits for them, and re-layouts  14.8 us
    pallas_call x4, Pallas kernels, dequantize_pieces(): pl.pallas_call(functools.partial(scale_body, block), out_shape=jax.ShapeD...  13.8 us
  transfers between devices with their start and end apart: 42, of which 16 were waited for; matrix products, arithmetic and copies ran while one was open for 30% of the time, Pallas kernels for 10%

profile of v1, /device:TPU:0, one launch (start us, length us, event | category | flops | bytes accessed | tf_op | source)
XLA Modules:
  0.0 277.2 jit_solution(14551409113373582533)
XLA Ops:
  0.7 3.3 %fusion.6 = (bf16[128,896]{1,0:T(8,128)(2,1)S(1)}, bf16[128,896]{1,0:T(8,128)(2,1)S(1)}, bf16[128,896]{1,0:T(8,128)(2,1)S(1)}, bf16[128,896]{1,0:T(8,128)(2,1)S(...) fusion(bf16[128,7168]{1,0:T(8,128)(2,1)} %param.6, ...), kind=kLoop, calls=%fused_computation.118 | loop fusion | flops 7340032 | bytes 5505056 | tf_op jit(solution)/shard_map/convert_element_type | solution.py:188
  5.0 3.0 %collective-permute-start = (bf16[128,3584]{1,0:T(8,128)(2,1)}, bf16[128,3584]{1,0:T(8,128)(2,1)S(1)}, u32[]{:S(2)}, u32[]{:S(2)}) collective-permute-start(bf16[128,3584]{1,0:T(8,128)(2,1)} %pad_maximum_fusion.8), channel_id=1, source_target_pairs={{0,2},{2,0},{1,3},{3,1},{4,6},{6,4},{5,7},{7,5},{8,10},{10,8},{9,1... | collective-permute-start | bytes 2752520 | tf_op jit(solution)/shard_map/ppermute | solution.py:125
  9.3 1.6 collective-permute-start.1
  11.0 2.3 collective-permute-start.10
  16.4 3.2 %shard_map.84 = bf16[512,896]{1,0:T(8,128)(2,1)} custom-call(s32[2]{0:T(128)} %pad_add_fusion.1.index_ref, bf16[512,7168]{1,0:T(8,128)(2,1)} %codes_ref.5, bf16[512,56]{1,0:T(8,128)(2,1)} %copy.14.scales_ref), custom_call_target="tpu_custom_call" | custom-call | flops 458752 | bytes 1835008 | tf_op jit(solution)/shard_map/pallas_call | solution.py:86
  23.4 3.4 %shard_map.87 = bf16[512,896]{1,0:T(8,128)(2,1)} custom-call(s32[2]{0:T(128)} %pad_add_fusion.index_ref, bf16[512,7168]{1,0:T(8,128)(2,1)} %codes_ref.5, bf16[512,56]{1,0:T(8,128)(2,1)} %copy.14.scales_ref), custom_call_target="tpu_custom_call" | custom-call | flops 458752 | bytes 1835008 | tf_op jit(solution)/shard_map/pallas_call | solution.py:86
  27.5 5.7 %collective-permute-start.2 = (bf16[128,3584]{1,0:T(8,128)(2,1)}, bf16[128,3584]{1,0:T(8,128)(2,1)S(1)}, u32[]{:S(2)}, u32[]{:S(2)}) collective-permute-start(bf16[128,3584]{1,0:T(8,128)(2,1)} %get-tuple-element.44), channel_id=1, source_target_pairs={{0,4},{4,8},{8,12},{1,5},{5,9},{9,13},{2,6},{6,10},{10,14},{3,7},{... | collective-permute-start | bytes 2752520 | tf_op jit(solution)/shard_map/ppermute | solution.py:142
  33.2 3.6 %shard_map.85 = bf16[1024,1792]{1,0:T(8,128)(2,1)} custom-call(s32[3]{0:T(128)} %add_add_fusion.index_ref, bf16[512,7168]{1,0:T(8,128)(2,1)} %codes_ref.5, bf16[512,56]{1,0:T(8,128)(2,1)} %copy.14.scales_ref), custom_call_target="tpu_custom_call" | custom-call | flops 917504 | bytes 3670016 | tf_op jit(solution)/shard_map/pallas_call | solution.py:86
  36.8 3.6 %shard_map.86 = bf16[1024,1792]{1,0:T(8,128)(2,1)} custom-call(s32[3]{0:T(128)} %add_add_fusion.1.index_ref, bf16[512,7168]{1,0:T(8,128)(2,1)} %codes_ref.5, bf16[512,56]{1,0:T(8,128)(2,1)} %copy.14.scales_ref), custom_call_target="tpu_custom_call" | custom-call | flops 917504 | bytes 3670016 | tf_op jit(solution)/shard_map/pallas_call | solution.py:86
  43.2 5.1 %collective-permute-done.11 = bf16[512,896]{1,0:T(8,128)(2,1)} collective-permute-done((bf16[512,896]{1,0:T(8,128)(2,1)}, bf16[512,896]{1,0:T(8,128)(2,1)}, u32[]{:S(2)}, u32[]{:S(2)}) %collective-permute-start.11) | collective-permute-done | bytes 917536 | tf_op jit(solution)/shard_map/ppermute | solution.py:125
  48.3 1.7 collective-permute-start.16
  53.9 7.2 %collective-permute-done.3 = bf16[128,3584]{1,0:T(8,128)(2,1)S(1)} collective-permute-done((bf16[128,3584]{1,0:T(8,128)(2,1)}, bf16[128,3584]{1,0:T(8,128)(2,1)S(1)}, u32[]{:S(2)}, u32[]{:S(2)}) %collective-permute-start.3) | collective-permute-done | bytes 917536 | tf_op jit(solution)/shard_map/ppermute | solution.py:142
  61.1 3.1 %collective-permute-start.4 = (bf16[128,3584]{1,0:T(8,128)(2,1)S(1)}, bf16[128,3584]{1,0:T(8,128)(2,1)S(1)}, u32[]{:S(2)}, u32[]{:S(2)}) collective-permute-start(bf16[128,3584]{1,0:T(8,128)(2,1)S(1)} %collective-permute-done), channel_id=1, source_target_pairs={{0,4},{4,8},{8,12},{1,5},{5,9},{9,13},{2,6},{6,10},{10,14},{3,7},{... | collective-permute-start | bytes 2752520 | tf_op jit(solution)/shard_map/ppermute | solution.py:142
  67.5 2.6 collective-permute-done.16
  71.6 6.4 %collective-permute-done.4 = bf16[128,3584]{1,0:T(8,128)(2,1)S(1)} collective-permute-done((bf16[128,3584]{1,0:T(8,128)(2,1)S(1)}, bf16[128,3584]{1,0:T(8,128)(2,1)S(1)}, u32[]{:S(2)}, u32[]{:S(2)}) %collective-permute-start.4) | collective-permute-done | bytes 917536 | tf_op jit(solution)/shard_map/ppermute | solution.py:142
  78.8 5.7 %collective-permute-done.5 = bf16[128,3584]{1,0:T(8,128)(2,1)S(1)} collective-permute-done((bf16[128,3584]{1,0:T(8,128)(2,1)S(1)}, bf16[128,3584]{1,0:T(8,128)(2,1)S(1)}, u32[]{:S(2)}, u32[]{:S(2)}) %collective-permute-start.5) | collective-permute-done | bytes 917536 | tf_op jit(solution)/shard_map/ppermute | solution.py:142
  90.8 4.2 %convolution_convert_fusion.1 = bf16[1024,1792]{1,0:T(8,128)(2,1)S(1)} fusion(bf16[1024,1024]{1,0:T(8,128)(2,1)S(1)} %bitcast.112, bf16[1024,1792]{1,0:T(8,128)(2,1)S(1)} %constant_dynamic-update-slice_fusion.26.refs_0_), kind=kOutput, calls=%fused_computation.3 | convolution fusion | flops 3759931392 | bytes 9437184 | tf_op jit(solution)/shard_map/dot_general | solution.py:14
  95.0 2.3 dynamic-slice_bitcast_fusion.7
  98.2 5.5 %collective-permute-start.22 = (bf16[256,1792]{1,0:T(8,128)(2,1)}, bf16[256,1792]{1,0:T(8,128)(2,1)}, u32[]{:S(2)}, u32[]{:S(2)}) collective-permute-start(bf16[256,1792]{1,0:T(8,128)(2,1)} %get-tuple-element.93), channel_id=1, source_target_pairs={{0,4},{12,8},{1,5},{13,9},{2,6},{14,10},{3,7},{15,11},{16,20},{28,... | collective-permute-start | bytes 2752520 | tf_op jit(solution)/shard_map/ppermute | solution.py:148
  103.8 2.3 collective-permute-done.14
  107.3 2.5 collective-permute-start.17
  111.1 4.2 %convolution_convert_fusion = bf16[1024,1792]{1,0:T(8,128)(2,1)S(1)} fusion(bf16[1024,1024]{1,0:T(8,128)(2,1)S(1)} %bitcast.113, bf16[1024,1792]{1,0:T(8,128)(2,1)S(1)} %constant_dynamic-update-slice_fusion.25.refs_1_), kind=kOutput, calls=%fused_computation.2 | convolution fusion | flops 3759931392 | bytes 9437184 | tf_op jit(solution)/shard_map/dot_general | solution.py:14
  116.4 2.4 dynamic-slice_bitcast_fusion.6
  118.8 5.6 %collective-permute-start.23 = (bf16[256,1792]{1,0:T(8,128)(2,1)}, bf16[256,1792]{1,0:T(8,128)(2,1)}, u32[]{:S(2)}, u32[]{:S(2)}) collective-permute-start(bf16[256,1792]{1,0:T(8,128)(2,1)} %get-tuple-element.98), channel_id=1, source_target_pairs={{0,4},{12,8},{1,5},{13,9},{2,6},{14,10},{3,7},{15,11},{16,20},{28,... | collective-permute-start | bytes 2752520 | tf_op jit(solution)/shard_map/ppermute | solution.py:148
  131.4 3.8 %collective-permute-done.23 = bf16[256,1792]{1,0:T(8,128)(2,1)} collective-permute-done((bf16[256,1792]{1,0:T(8,128)(2,1)}, bf16[256,1792]{1,0:T(8,128)(2,1)}, u32[]{:S(2)}, u32[]{:S(2)}) %collective-permute-start.23) | collective-permute-done | bytes 917536 | tf_op jit(solution)/shard_map/ppermute | solution.py:148
  137.9 1.7 maximum_add_fusion.1
  139.6 5.6 %collective-permute-start.24 = (bf16[256,3584]{1,0:T(8,128)(2,1)}, bf16[256,3584]{1,0:T(8,128)(2,1)}, u32[]{:S(2)}, u32[]{:S(2)}) collective-permute-start(bf16[256,3584]{1,0:T(8,128)(2,1)} %maximum_add_fusion.1), channel_id=1, source_target_pairs={{0,4},{4,8},{1,5},{5,9},{2,6},{6,10},{3,7},{7,11},{16,20},{20,24},... | collective-permute-start | bytes 5505032 | tf_op jit(solution)/shard_map/ppermute | solution.py:142
  145.3 1.7 maximum_add_fusion.3
  146.9 1.9 collective-permute-start.25
  148.8 2.2 constant_dynamic-update-slice_fusion.15
  154.9 6.0 %collective-permute-done.8 = bf16[256,3584]{1,0:T(8,128)(2,1)} collective-permute-done((bf16[256,3584]{1,0:T(8,128)(2,1)}, bf16[256,3584]{1,0:T(8,128)(2,1)}, u32[]{:S(2)}, u32[]{:S(2)}) %collective-permute-start.8) | collective-permute-done | bytes 1835040 | tf_op jit(solution)/shard_map/ppermute | solution.py:148
  160.9 1.7 broadcast_select_fusion.1
  166.5 12.9 %shard_map.88 = bf16[1024,1024]{1,0:T(8,128)(2,1)S(1)} custom-call(bf16[1024,3584]{1,0:T(8,128)(2,1)S(1)} %get-tuple-element.64.left_ref, bf16[1024,1792]{1,0:T(8,128)(2,1)S(1)} %constant_dynamic-update-slice_fusion.26.refs_0_, bf16[1024,1792]{1,0:T(8,128)(2,1)S(1)} %constant_dynamic-update-slice_fusion.25.refs_1_), custom_call_target="tpu_custom_call" | custom-call | flops 7516192768 | bytes 29360128 | tf_op jit(solution)/shard_map/pallas_call | solution.py:46
  180.9 2.0 maximum_add_fusion
  183.0 1.9 maximum_add_fusion.2
  191.3 1.7 collective-permute-start.21
  197.1 8.5 %multiply_convert_fusion = bf16[1024,1792]{1,0:T(8,128)(2,1)S(1)} fusion(bf16[2048,1024]{1,0:T(8,128)(2,1)S(1)} %bitcast.109, bf16[2048,1792]{1,0:T(8,128)(2,1)S(1)} %bitcast.121), kind=kOutput, calls=%fused_computation | convolution fusion | flops 7519862784 | bytes 15204352 | tf_op jit(solution)/shard_map/dot_general | solution.py:14
  205.7 4.3 %collective-permute-start.30 = (bf16[256,1792]{1,0:T(8,128)(2,1)}, bf16[256,1792]{1,0:T(8,128)(2,1)}, u32[]{:S(2)}, u32[]{:S(2)}) collective-permute-start(bf16[256,1792]{1,0:T(8,128)(2,1)} %get-tuple-element.69), channel_id=1, source_target_pairs={{0,4},{4,8},{8,12},{1,5},{5,9},{9,13},{2,6},{6,10},{10,14},{3,7},{... | collective-permute-start | bytes 2752520 | tf_op jit(solution)/shard_map/ppermute | solution.py:142
  214.4 1.8 collective-permute-start.38
  218.4 9.8 %collective-permute-done.30 = bf16[256,1792]{1,0:T(8,128)(2,1)} collective-permute-done((bf16[256,1792]{1,0:T(8,128)(2,1)}, bf16[256,1792]{1,0:T(8,128)(2,1)}, u32[]{:S(2)}, u32[]{:S(2)}) %collective-permute-start.30) | collective-permute-done | bytes 917536 | tf_op jit(solution)/shard_map/ppermute | solution.py:142
  228.1 5.0 %collective-permute-done.31 = bf16[256,1792]{1,0:T(8,128)(2,1)} collective-permute-done((bf16[256,1792]{1,0:T(8,128)(2,1)}, bf16[256,1792]{1,0:T(8,128)(2,1)}, u32[]{:S(2)}, u32[]{:S(2)}) %collective-permute-start.31) | collective-permute-done | bytes 917536 | tf_op jit(solution)/shard_map/ppermute | solution.py:142
  236.3 1.6 collective-permute-done.38
  238.0 2.1 add_convert_fusion.1
  243.7 11.4 %collective-permute-done.39 = bf16[256,1792]{1,0:T(8,128)(2,1)S(1)} collective-permute-done((bf16[256,1792]{1,0:T(8,128)(2,1)}, bf16[256,1792]{1,0:T(8,128)(2,1)S(1)}, u32[]{:S(2)}, u32[]{:S(2)}) %collective-permute-start.39) | collective-permute-done | bytes 917536 | tf_op jit(solution)/shard_map/ppermute | solution.py:133
  255.7 1.6 collective-permute-done.33
  257.4 2.9 %collective-permute-start.34 = (bf16[64,1024]{1,0:T(8,128)(2,1)S(1)}, bf16[64,1024]{1,0:T(8,128)(2,1)S(1)}, u32[]{:S(2)}, u32[]{:S(2)}) collective-permute-start(bf16[64,1024]{1,0:T(8,128)(2,1)S(1)} %get-tuple-element.173), channel_id=1, source_target_pairs={{0,12},{4,0},{8,4},{12,8},{1,13},{5,1},{9,5},{13,9},{2,14},{6,2},{... | collective-permute-start | bytes 393224 | tf_op jit(solution)/shard_map/ppermute | solution.py:125
  265.7 5.0 %collective-permute-done.35 = bf16[64,1024]{1,0:T(8,128)(2,1)S(1)} collective-permute-done((bf16[64,1024]{1,0:T(8,128)(2,1)S(1)}, bf16[64,1024]{1,0:T(8,128)(2,1)S(1)}, u32[]{:S(2)}, u32[]{:S(2)}) %collective-permute-start.35) | collective-permute-done | bytes 131104 | tf_op jit(solution)/shard_map/ppermute | solution.py:125
  270.8 3.8 %collective-permute-done.41 = bf16[128,1792]{1,0:T(8,128)(2,1)S(1)} collective-permute-done((bf16[128,1792]{1,0:T(8,128)(2,1)S(1)}, bf16[128,1792]{1,0:T(8,128)(2,1)S(1)}, u32[]{:S(2)}, u32[]{:S(2)}) %collective-permute-start.41) | collective-permute-done | bytes 458784 | tf_op jit(solution)/shard_map/ppermute | solution.py:125
  (204 shorter events, 84.0 us)
Async XLA Ops:
  5.0 38.0 %collective-permute-start = (bf16[128,3584]{1,0:T(8,128)(2,1)}, bf16[128,3584]{1,0:T(8,128)(2,1)S(1)}, u32[]{:S(2)}, u32[]{:S(2)}) collective-permute-start(bf16[128,3584]{1,0:T(8,128)(2,1)} %pad_maximum_fusion.8), channel_id=1, source_target_pairs={{0,2},{2,0},{1,3},{3,1},{4,6},{6,4},{5,7},{7,5},{8,10},{10,8},{9,1... | collective-permute-start | bytes 2752520 | tf_op jit(solution)/shard_map/ppermute | solution.py:125
  9.3 17.5 %collective-permute-start.1 = (bf16[64,2048]{1,0:T(8,128)(2,1)S(1)}, bf16[64,2048]{1,0:T(8,128)(2,1)S(1)}, u32[]{:S(2)}, u32[]{:S(2)}) collective-permute-start(bf16[64,2048]{1,0:T(8,128)(2,1)S(1)} %pad_maximum_fusion.18), channel_id=1, source_target_pairs={{0,4},{4,8},{8,12},{12,0},{1,5},{5,9},{9,13},{13,1},{2,6},{6,10},{... | collective-permute-start | bytes 786440 | tf_op jit(solution)/shard_map/ppermute | solution.py:125
  11.0 29.4 %collective-permute-start.10 = (bf16[64,2048]{1,0:T(8,128)(2,1)S(1)}, bf16[64,2048]{1,0:T(8,128)(2,1)}, u32[]{:S(2)}, u32[]{:S(2)}) collective-permute-start(bf16[64,2048]{1,0:T(8,128)(2,1)S(1)} %pad_maximum_fusion.20), channel_id=1, source_target_pairs={{0,12},{4,0},{8,4},{12,8},{1,13},{5,1},{9,5},{13,9},{2,14},{6,2},{... | collective-permute-start | bytes 786440 | tf_op jit(solution)/shard_map/ppermute | solution.py:125
  13.3 28.4 %collective-permute-start.9 = (bf16[64,2048]{1,0:T(8,128)(2,1)S(1)}, bf16[64,2048]{1,0:T(8,128)(2,1)}, u32[]{:S(2)}, u32[]{:S(2)}) collective-permute-start(bf16[64,2048]{1,0:T(8,128)(2,1)S(1)} %pad_maximum_fusion.19), channel_id=1, source_target_pairs={{0,8},{4,12},{8,0},{12,4},{1,9},{5,13},{9,1},{13,5},{2,10},{6,14},... | collective-permute-start | bytes 786440 | tf_op jit(solution)/shard_map/ppermute | solution.py:125
  19.6 28.7 %collective-permute-start.11 = (bf16[512,896]{1,0:T(8,128)(2,1)}, bf16[512,896]{1,0:T(8,128)(2,1)}, u32[]{:S(2)}, u32[]{:S(2)}) collective-permute-start(bf16[512,896]{1,0:T(8,128)(2,1)} %shard_map.84), channel_id=1, source_target_pairs={{0,2},{2,0},{1,3},{3,1},{4,6},{6,4},{5,7},{7,5},{8,10},{10,8},{9,1... | collective-permute-start | bytes 2752520 | tf_op jit(solution)/shard_map/ppermute | solution.py:125
  27.5 26.4 %collective-permute-start.2 = (bf16[128,3584]{1,0:T(8,128)(2,1)}, bf16[128,3584]{1,0:T(8,128)(2,1)S(1)}, u32[]{:S(2)}, u32[]{:S(2)}) collective-permute-start(bf16[128,3584]{1,0:T(8,128)(2,1)} %get-tuple-element.44), channel_id=1, source_target_pairs={{0,4},{4,8},{8,12},{1,5},{5,9},{9,13},{2,6},{6,10},{10,14},{3,7},{... | collective-permute-start | bytes 2752520 | tf_op jit(solution)/shard_map/ppermute | solution.py:142
  40.4 20.7 %collective-permute-start.3 = (bf16[128,3584]{1,0:T(8,128)(2,1)}, bf16[128,3584]{1,0:T(8,128)(2,1)S(1)}, u32[]{:S(2)}, u32[]{:S(2)}) collective-permute-start(bf16[128,3584]{1,0:T(8,128)(2,1)} %get-tuple-element.44), channel_id=1, source_target_pairs={{12,8},{8,4},{4,0},{13,9},{9,5},{5,1},{14,10},{10,6},{6,2},{15,11}... | collective-permute-start | bytes 2752520 | tf_op jit(solution)/shard_map/ppermute | solution.py:142
  43.1 8.5 %copy-start.1 = (bf16[1024,1792]{1,0:T(8,128)(2,1)S(1)}, bf16[1024,1792]{1,0:T(8,128)(2,1)}, u32[]{:S(2)}) copy-start(bf16[1024,1792]{1,0:T(8,128)(2,1)} %shard_map.85) | copy-start | bytes 11010052
  48.3 21.7 %collective-permute-start.16 = (bf16[512,896]{1,0:T(8,128)(2,1)}, bf16[512,896]{1,0:T(8,128)(2,1)S(1)}, u32[]{:S(2)}, u32[]{:S(2)}) collective-permute-start(bf16[512,896]{1,0:T(8,128)(2,1)} %collective-permute-done.11), channel_id=1, source_target_pairs={{0,16},{16,0},{1,17},{17,1},{2,18},{18,2},{3,19},{19,3},{4,20},{20... | collective-permute-start | bytes 2752520 | tf_op jit(solution)/shard_map/ppermute | solution.py:125
  50.0 15.6 %collective-permute-start.12 = (bf16[4,64,1024]{2,1,0:T(8,128)(2,1)S(1)}, bf16[4,64,1024]{2,1,0:T(8,128)(2,1)S(1)}, u32[]{:S(2)}, u32[]{:S(2)}) collective-permute-start(bf16[4,64,1024]{2,1,0:T(8,128)(2,1)S(1)} %get-tuple-element.57), channel_id=1, source_target_pairs={{0,2},{2,0},{1,3},{3,1},{4,6},{6,4},{5,7},{7,5},{8,10},{10,8},{9,1... | collective-permute-start | bytes 1572872 | tf_op jit(solution)/shard_map/ppermute | solution.py:125
  53.9 11.8 %copy-start.19 = (bf16[512,896]{1,0:T(8,128)(2,1)S(1)}, bf16[512,896]{1,0:T(8,128)(2,1)}, u32[]{:S(2)}) copy-start(bf16[512,896]{1,0:T(8,128)(2,1)} %shard_map.87) | copy-start | bytes 2752516
  61.1 16.9 %collective-permute-start.4 = (bf16[128,3584]{1,0:T(8,128)(2,1)S(1)}, bf16[128,3584]{1,0:T(8,128)(2,1)S(1)}, u32[]{:S(2)}, u32[]{:S(2)}) collective-permute-start(bf16[128,3584]{1,0:T(8,128)(2,1)S(1)} %collective-permute-done), channel_id=1, source_target_pairs={{0,4},{4,8},{8,12},{1,5},{5,9},{9,13},{2,6},{6,10},{10,14},{3,7},{... | collective-permute-start | bytes 2752520 | tf_op jit(solution)/shard_map/ppermute | solution.py:142
  64.2 20.3 %collective-permute-start.5 = (bf16[128,3584]{1,0:T(8,128)(2,1)S(1)}, bf16[128,3584]{1,0:T(8,128)(2,1)S(1)}, u32[]{:S(2)}, u32[]{:S(2)}) collective-permute-start(bf16[128,3584]{1,0:T(8,128)(2,1)S(1)} %collective-permute-done), channel_id=1, source_target_pairs={{12,8},{8,4},{4,0},{13,9},{9,5},{5,1},{14,10},{10,6},{6,2},{15,11}... | collective-permute-start | bytes 2752520 | tf_op jit(solution)/shard_map/ppermute | solution.py:142
  65.6 20.3 %slice-start = ((s8[7340032]{0:T(1024)(128)(4,1)}), s8[4194304]{0:T(1024)(128)(4,1)S(1)}, s32[]{:S(2)}) async-start(s8[7340032]{0:T(1024)(128)(4,1)} %bitcast.103), calls=%async_computation | async-start | bytes 8388608
  65.7 22.2 %collective-permute-start.13 = (bf16[512,896]{1,0:T(8,128)(2,1)S(1)}, bf16[512,896]{1,0:T(8,128)(2,1)}, u32[]{:S(2)}, u32[]{:S(2)}) collective-permute-start(bf16[512,896]{1,0:T(8,128)(2,1)S(1)} %copy-done.19), channel_id=1, source_target_pairs={{0,2},{2,0},{1,3},{3,1},{4,6},{6,4},{5,7},{7,5},{8,10},{10,8},{9,1... | collective-permute-start | bytes 2752520 | tf_op jit(solution)/shard_map/ppermute | solution.py:125
  67.0 23.6 %collective-permute-start.15 = (bf16[4,2,64,1024]{3,2,1,0:T(8,128)(2,1)S(1)}, bf16[4,2,64,1024]{3,2,1,0:T(8,128)(2,1)S(1)}, u32[]{:S(2)}, u32[]{:S(2)}) collective-permute-start(bf16[4,2,64,1024]{3,2,1,0:T(8,128)(2,1)S(1)} %pad_maximum_fusion.6), channel_id=1, source_target_pairs={{0,1},{1,0},{2,3},{3,2},{4,5},{5,4},{6,7},{7,6},{8,9},{9,8},{10,11... | collective-permute-start | bytes 3145736 | tf_op jit(solution)/shard_map/ppermute | solution.py:125
  67.4 18.5 %slice-start.1 = ((s8[7340032]{0:T(1024)(128)(4,1)}), s8[3145728]{0:T(1024)(128)(4,1)S(1)}, s32[]{:S(2)}) async-start(s8[7340032]{0:T(1024)(128)(4,1)} %bitcast.103), calls=%async_computation.1 | async-start | bytes 6291456
  70.1 16.3 %collective-permute-start.26 = (bf16[4,64,1024]{2,1,0:T(8,128)(2,1)S(1)}, bf16[4,64,1024]{2,1,0:T(8,128)(2,1)S(1)}, u32[]{:S(2)}, u32[]{:S(2)}) collective-permute-start(bf16[4,64,1024]{2,1,0:T(8,128)(2,1)S(1)} %get-tuple-element.67), channel_id=1, source_target_pairs={{0,16},{16,0},{1,17},{17,1},{2,18},{18,2},{3,19},{19,3},{4,20},{20... | collective-permute-start | bytes 1572872 | tf_op jit(solution)/shard_map/ppermute | solution.py:125
  78.0 47.9 %collective-permute-start.6 = (bf16[256,3584]{1,0:T(8,128)(2,1)S(1)}, bf16[256,3584]{1,0:T(8,128)(2,1)S(1)}, u32[]{:S(2)}, u32[]{:S(2)}) collective-permute-start(bf16[256,3584]{1,0:T(8,128)(2,1)S(1)} %constant_dynamic-update-slice_fusion), channel_id=1, source_target_pairs={{4,8},{8,12},{5,9},{9,13},{6,10},{10,14},{7,11},{11,15},{20,24},{2... | collective-permute-start | bytes 5505032 | tf_op jit(solution)/shard_map/ppermute | solution.py:142
  84.6 41.3 %collective-permute-start.7 = (bf16[256,3584]{1,0:T(8,128)(2,1)S(1)}, bf16[256,3584]{1,0:T(8,128)(2,1)S(1)}, u32[]{:S(2)}, u32[]{:S(2)}) collective-permute-start(bf16[256,3584]{1,0:T(8,128)(2,1)S(1)} %constant_dynamic-update-slice_fusion.2), channel_id=1, source_target_pairs={{8,4},{4,0},{9,5},{5,1},{10,6},{6,2},{11,7},{7,3},{24,20},{20,16},... | collective-permute-start | bytes 5505032 | tf_op jit(solution)/shard_map/ppermute | solution.py:142
  86.5 32.3 %collective-permute-start.27 = (bf16[4,2,64,1024]{3,2,0,1:T(8,128)(2,1)S(1)}, bf16[4,2,64,1024]{3,2,0,1:T(8,128)(2,1)S(1)}, u32[]{:S(2)}, u32[]{:S(2)}) collective-permute-start(bf16[4,2,64,1024]{3,2,0,1:T(8,128)(2,1)S(1)} %get-tuple-element.146), channel_id=1, source_target_pairs={{0,2},{2,0},{1,3},{3,1},{4,6},{6,4},{5,7},{7,5},{8,10},{10,8},{9,1... | collective-permute-start | bytes 3145736 | tf_op jit(solution)/shard_map/ppermute | solution.py:125
  87.8 18.3 %collective-permute-start.14 = (bf16[512,896]{1,0:T(8,128)(2,1)}, bf16[512,896]{1,0:T(8,128)(2,1)}, u32[]{:S(2)}, u32[]{:S(2)}) collective-permute-start(bf16[512,896]{1,0:T(8,128)(2,1)} %collective-permute-done.13), channel_id=1, source_target_pairs={{0,16},{16,0},{1,17},{17,1},{2,18},{18,2},{3,19},{19,3},{4,20},{20... | collective-permute-start | bytes 2752520 | tf_op jit(solution)/shard_map/ppermute | solution.py:125
  98.2 26.4 %collective-permute-start.22 = (bf16[256,1792]{1,0:T(8,128)(2,1)}, bf16[256,1792]{1,0:T(8,128)(2,1)}, u32[]{:S(2)}, u32[]{:S(2)}) collective-permute-start(bf16[256,1792]{1,0:T(8,128)(2,1)} %get-tuple-element.93), channel_id=1, source_target_pairs={{0,4},{12,8},{1,5},{13,9},{2,6},{14,10},{3,7},{15,11},{16,20},{28,... | collective-permute-start | bytes 2752520 | tf_op jit(solution)/shard_map/ppermute | solution.py:148
  107.3 22.3 %collective-permute-start.17 = (bf16[256,1792]{1,0:T(8,128)(2,1)}, bf16[256,1792]{1,0:T(8,128)(2,1)}, u32[]{:S(2)}, u32[]{:S(2)}) collective-permute-start(bf16[256,1792]{1,0:T(8,128)(2,1)} %pad_maximum_fusion.11), channel_id=1, source_target_pairs={{0,16},{16,0},{1,17},{17,1},{2,18},{18,2},{3,19},{19,3},{4,20},{20... | collective-permute-start | bytes 2752520 | tf_op jit(solution)/shard_map/ppermute | solution.py:125
  118.8 16.3 %collective-permute-start.23 = (bf16[256,1792]{1,0:T(8,128)(2,1)}, bf16[256,1792]{1,0:T(8,128)(2,1)}, u32[]{:S(2)}, u32[]{:S(2)}) collective-permute-start(bf16[256,1792]{1,0:T(8,128)(2,1)} %get-tuple-element.98), channel_id=1, source_target_pairs={{0,4},{12,8},{1,5},{13,9},{2,6},{14,10},{3,7},{15,11},{16,20},{28,... | collective-permute-start | bytes 2752520 | tf_op jit(solution)/shard_map/ppermute | solution.py:148
  128.3 32.6 %collective-permute-start.8 = (bf16[256,3584]{1,0:T(8,128)(2,1)}, bf16[256,3584]{1,0:T(8,128)(2,1)}, u32[]{:S(2)}, u32[]{:S(2)}) collective-permute-start(bf16[256,3584]{1,0:T(8,128)(2,1)} %broadcast_select_fusion), channel_id=1, source_target_pairs={{8,12},{4,0},{9,13},{5,1},{10,14},{6,2},{11,15},{7,3},{24,28},{20,... | collective-permute-start | bytes 5505032 | tf_op jit(solution)/shard_map/ppermute | solution.py:148
  130.8 21.2 %collective-permute-start.18 = (bf16[256,1792]{1,0:T(8,128)(2,1)}, bf16[256,1792]{1,0:T(8,128)(2,1)S(1)}, u32[]{:S(2)}, u32[]{:S(2)}) collective-permute-start(bf16[256,1792]{1,0:T(8,128)(2,1)} %pad_maximum_fusion.13), channel_id=1, source_target_pairs={{0,16},{16,0},{1,17},{17,1},{2,18},{18,2},{3,19},{19,3},{4,20},{20... | collective-permute-start | bytes 2752520 | tf_op jit(solution)/shard_map/ppermute | solution.py:125
  137.9 7.4 %copy-start.14 = (bf16[256,1792]{1,0:T(8,128)(2,1)S(1)}, bf16[256,1792]{1,0:T(8,128)(2,1)}, u32[]{:S(2)}) copy-start(bf16[256,1792]{1,0:T(8,128)(2,1)} %get-tuple-element.97) | copy-start | bytes 2752516
  139.6 40.1 %collective-permute-start.24 = (bf16[256,3584]{1,0:T(8,128)(2,1)}, bf16[256,3584]{1,0:T(8,128)(2,1)}, u32[]{:S(2)}, u32[]{:S(2)}) collective-permute-start(bf16[256,3584]{1,0:T(8,128)(2,1)} %maximum_add_fusion.1), channel_id=1, source_target_pairs={{0,4},{4,8},{1,5},{5,9},{2,6},{6,10},{3,7},{7,11},{16,20},{20,24},... | collective-permute-start | bytes 5505032 | tf_op jit(solution)/shard_map/ppermute | solution.py:142
  146.9 36.1 %collective-permute-start.25 = (bf16[256,3584]{1,0:T(8,128)(2,1)}, bf16[256,3584]{1,0:T(8,128)(2,1)}, u32[]{:S(2)}, u32[]{:S(2)}) collective-permute-start(bf16[256,3584]{1,0:T(8,128)(2,1)} %maximum_add_fusion.3), channel_id=1, source_target_pairs={{12,8},{8,4},{13,9},{9,5},{14,10},{10,6},{15,11},{11,7},{28,24},{2... | collective-permute-start | bytes 5505032 | tf_op jit(solution)/shard_map/ppermute | solution.py:142
  152.3 13.5 %collective-permute-start.19 = (bf16[256,1792]{1,0:T(8,128)(2,1)S(1)}, bf16[256,1792]{1,0:T(8,128)(2,1)S(1)}, u32[]{:S(2)}, u32[]{:S(2)}) collective-permute-start(bf16[256,1792]{1,0:T(8,128)(2,1)S(1)} %pad_maximum_fusion.15), channel_id=1, source_target_pairs={{0,16},{16,0},{1,17},{17,1},{2,18},{18,2},{3,19},{19,3},{4,20},{20... | collective-permute-start | bytes 2752520 | tf_op jit(solution)/shard_map/ppermute | solution.py:125
  162.6 30.4 %collective-permute-start.28 = (bf16[4,2,2,64,1024]{4,3,0,1,2:T(8,128)(2,1)S(1)}, bf16[4,2,2,64,1024]{4,3,0,1,2:T(8,128)(2,1)S(1)}, u32[]{:S(2)}, u32[]{:S(2)}) collective-permute-start(bf16[4,2,2,64,1024]{4,3,0,1,2:T(8,128)(2,1)S(1)} %pad_maximum_fusion.1), channel_id=1, source_target_pairs={{0,1},{1,0},{2,3},{3,2},{4,5},{5,4},{6,7},{7,6},{8,9},{9,8},{10,11... | collective-permute-start | bytes 6291464 | tf_op jit(solution)/shard_map/ppermute | solution.py:125
  166.0 23.1 %collective-permute-start.29 = (bf16[256,1792]{1,0:T(8,128)(2,1)S(1)}, bf16[256,1792]{1,0:T(8,128)(2,1)S(1)}, u32[]{:S(2)}, u32[]{:S(2)}) collective-permute-start(bf16[256,1792]{1,0:T(8,128)(2,1)S(1)} %pad_maximum_fusion.17), channel_id=1, source_target_pairs={{0,16},{16,0},{1,17},{17,1},{2,18},{18,2},{3,19},{19,3},{4,20},{20... | collective-permute-start | bytes 2752520 | tf_op jit(solution)/shard_map/ppermute | solution.py:125
  179.6 10.5 %collective-permute-start.20 = (bf16[4,2,64,1024]{3,2,1,0:T(8,128)(2,1)S(1)}, bf16[4,2,64,1024]{3,2,1,0:T(8,128)(2,1)S(1)}, u32[]{:S(2)}, u32[]{:S(2)}) collective-permute-start(bf16[4,2,64,1024]{3,2,1,0:T(8,128)(2,1)S(1)} %dynamic-slice_bitcast_fusion), channel_id=1, source_target_pairs={{0,1},{1,0},{2,3},{3,2},{4,5},{5,4},{6,7},{7,6},{8,9},{9,8},{10,11... | collective-permute-start | bytes 3145736 | tf_op jit(solution)/shard_map/ppermute | solution.py:125
  191.3 24.8 %collective-permute-start.21 = (bf16[4,64,1024]{2,1,0:T(8,128)(2,1)}, bf16[4,64,1024]{2,1,0:T(8,128)(2,1)S(1)}, u32[]{:S(2)}, u32[]{:S(2)}) collective-permute-start(bf16[4,64,1024]{2,1,0:T(8,128)(2,1)} %slice_bitcast_fusion), channel_id=1, source_target_pairs={{0,2},{2,0},{1,3},{3,1},{4,6},{6,4},{5,7},{7,5},{8,10},{10,8},{9,1... | collective-permute-start | bytes 1572872 | tf_op jit(solution)/shard_map/ppermute | solution.py:125
  205.7 22.4 %collective-permute-start.30 = (bf16[256,1792]{1,0:T(8,128)(2,1)}, bf16[256,1792]{1,0:T(8,128)(2,1)}, u32[]{:S(2)}, u32[]{:S(2)}) collective-permute-start(bf16[256,1792]{1,0:T(8,128)(2,1)} %get-tuple-element.69), channel_id=1, source_target_pairs={{0,4},{4,8},{8,12},{1,5},{5,9},{9,13},{2,6},{6,10},{10,14},{3,7},{... | collective-permute-start | bytes 2752520 | tf_op jit(solution)/shard_map/ppermute | solution.py:142
  210.0 23.2 %collective-permute-start.31 = (bf16[256,1792]{1,0:T(8,128)(2,1)}, bf16[256,1792]{1,0:T(8,128)(2,1)}, u32[]{:S(2)}, u32[]{:S(2)}) collective-permute-start(bf16[256,1792]{1,0:T(8,128)(2,1)} %get-tuple-element.70), channel_id=1, source_target_pairs={{12,8},{8,4},{4,0},{13,9},{9,5},{5,1},{14,10},{10,6},{6,2},{15,11}... | collective-permute-start | bytes 2752520 | tf_op jit(solution)/shard_map/ppermute | solution.py:142
  212.9 23.4 %collective-permute-start.37 = (bf16[256,1792]{1,0:T(8,128)(2,1)}, bf16[256,1792]{1,0:T(8,128)(2,1)}, u32[]{:S(2)}, u32[]{:S(2)}) collective-permute-start(bf16[256,1792]{1,0:T(8,128)(2,1)} %get-tuple-element.90), channel_id=1, source_target_pairs={{0,2},{2,0},{16,18},{18,16},{1,3},{3,1},{17,19},{19,17},{4,6},{6,4... | collective-permute-start | bytes 2752520 | tf_op jit(solution)/shard_map/ppermute | solution.py:133
  214.4 23.6 %collective-permute-start.38 = (bf16[256,1792]{1,0:T(8,128)(2,1)}, bf16[256,1792]{1,0:T(8,128)(2,1)}, u32[]{:S(2)}, u32[]{:S(2)}) collective-permute-start(bf16[256,1792]{1,0:T(8,128)(2,1)} %get-tuple-element.89), channel_id=1, source_target_pairs={{0,16},{2,18},{16,0},{18,2},{1,17},{3,19},{17,1},{19,3},{4,20},{6,... | collective-permute-start | bytes 2752520 | tf_op jit(solution)/shard_map/ppermute | solution.py:133
  216.4 38.7 %collective-permute-start.39 = (bf16[256,1792]{1,0:T(8,128)(2,1)}, bf16[256,1792]{1,0:T(8,128)(2,1)S(1)}, u32[]{:S(2)}, u32[]{:S(2)}) collective-permute-start(bf16[256,1792]{1,0:T(8,128)(2,1)} %get-tuple-element.88), channel_id=1, source_target_pairs={{0,18},{2,16},{16,2},{18,0},{1,19},{3,17},{17,3},{19,1},{4,22},{6,... | collective-permute-start | bytes 2752520 | tf_op jit(solution)/shard_map/ppermute | solution.py:133
  233.2 22.6 %collective-permute-start.32 = (bf16[256,1792]{1,0:T(8,128)(2,1)S(1)}, bf16[256,1792]{1,0:T(8,128)(2,1)S(1)}, u32[]{:S(2)}, u32[]{:S(2)}) collective-permute-start(bf16[256,1792]{1,0:T(8,128)(2,1)S(1)} %get-tuple-element.71), channel_id=1, source_target_pairs={{0,4},{4,8},{8,12},{1,5},{5,9},{9,13},{2,6},{6,10},{10,14},{3,7},{... | collective-permute-start | bytes 2752520 | tf_op jit(solution)/shard_map/ppermute | solution.py:142
  234.8 22.6 %collective-permute-start.33 = (bf16[256,1792]{1,0:T(8,128)(2,1)S(1)}, bf16[256,1792]{1,0:T(8,128)(2,1)S(1)}, u32[]{:S(2)}, u32[]{:S(2)}) collective-permute-start(bf16[256,1792]{1,0:T(8,128)(2,1)S(1)} %get-tuple-element.72), channel_id=1, source_target_pairs={{12,8},{8,4},{4,0},{13,9},{9,5},{5,1},{14,10},{10,6},{6,2},{15,11}... | collective-permute-start | bytes 2752520 | tf_op jit(solution)/shard_map/ppermute | solution.py:142
  240.1 24.8 %collective-permute-start.40 = (bf16[128,1792]{1,0:T(8,128)(2,1)S(1)}, bf16[128,1792]{1,0:T(8,128)(2,1)S(1)}, u32[]{:S(2)}, u32[]{:S(2)}) collective-permute-start(bf16[128,1792]{1,0:T(8,128)(2,1)S(1)} %slice.162), channel_id=1, source_target_pairs={{0,2},{2,0},{1,3},{3,1},{4,6},{6,4},{5,7},{7,5},{8,10},{10,8},{9,1... | collective-permute-start | bytes 1376264 | tf_op jit(solution)/shard_map/ppermute | solution.py:125
  243.6 11.7 %copy-start.5 = (bf16[128,7168]{1,0:T(8,128)(2,1)S(1)}, bf16[128,7168]{1,0:T(8,128)(2,1)}, u32[]{:S(2)}) copy-start(bf16[128,7168]{1,0:T(8,128)(2,1)} %param.6) | copy-start | bytes 5505028
  257.4 8.3 %collective-permute-start.34 = (bf16[64,1024]{1,0:T(8,128)(2,1)S(1)}, bf16[64,1024]{1,0:T(8,128)(2,1)S(1)}, u32[]{:S(2)}, u32[]{:S(2)}) collective-permute-start(bf16[64,1024]{1,0:T(8,128)(2,1)S(1)} %get-tuple-element.173), channel_id=1, source_target_pairs={{0,12},{4,0},{8,4},{12,8},{1,13},{5,1},{9,5},{13,9},{2,14},{6,2},{... | collective-permute-start | bytes 393224 | tf_op jit(solution)/shard_map/ppermute | solution.py:125
  260.3 10.4 %collective-permute-start.35 = (bf16[64,1024]{1,0:T(8,128)(2,1)S(1)}, bf16[64,1024]{1,0:T(8,128)(2,1)S(1)}, u32[]{:S(2)}, u32[]{:S(2)}) collective-permute-start(bf16[64,1024]{1,0:T(8,128)(2,1)S(1)} %get-tuple-element.172), channel_id=1, source_target_pairs={{0,8},{4,12},{8,0},{12,4},{1,9},{5,13},{9,1},{13,5},{2,10},{6,14},... | collective-permute-start | bytes 393224 | tf_op jit(solution)/shard_map/ppermute | solution.py:125
  260.8 9.9 %collective-permute-start.36 = (bf16[64,1024]{1,0:T(8,128)(2,1)S(1)}, bf16[64,1024]{1,0:T(8,128)(2,1)S(1)}, u32[]{:S(2)}, u32[]{:S(2)}) collective-permute-start(bf16[64,1024]{1,0:T(8,128)(2,1)S(1)} %get-tuple-element.171), channel_id=1, source_target_pairs={{0,4},{4,8},{8,12},{12,0},{1,5},{5,9},{9,13},{13,1},{2,6},{6,10},{... | collective-permute-start | bytes 393224 | tf_op jit(solution)/shard_map/ppermute | solution.py:125
  262.6 12.0 %collective-permute-start.41 = (bf16[128,1792]{1,0:T(8,128)(2,1)S(1)}, bf16[128,1792]{1,0:T(8,128)(2,1)S(1)}, u32[]{:S(2)}, u32[]{:S(2)}) collective-permute-start(bf16[128,1792]{1,0:T(8,128)(2,1)S(1)} %slice.165), channel_id=1, source_target_pairs={{0,2},{2,0},{1,3},{3,1},{4,6},{6,4},{5,7},{7,5},{8,10},{10,8},{9,1... | collective-permute-start | bytes 1376264 | tf_op jit(solution)/shard_map/ppermute | solution.py:125
  (22 other events, 62.7 us)
